TPU v7x, 32 devices: a whole 2x2x4 slice. The times are simulated.
32 devices in a mesh: rows: 16 (over z, y, x), seq: 2 (over core).
Axes of the slice: x: 2, y: 2, z: 4, core: 2. Of those that a mesh axis runs over, the one named last changes fastest.
Arguments:
- tokens: bfloat16 [16, 256, 768], P('rows', 'seq'), may hold values from -6 to 6
- marks: int32 [16, 256], P('rows', 'seq'), may hold values from 0 to 1, as said below
- norm_gain: float32 [768], replicated, may hold values from 0.5 to 1.5
- in_weight: bfloat16 [768, 3072], replicated, may hold values from -0.21875 to 0.21875
- conv_weight: float32 [4, 1536], replicated, may hold values from -3 to 3
- conv_bias: float32 [1536], replicated, may hold values from -3 to 3
- x_weight: bfloat16 [80, 1536], replicated, may hold values from -0.15625 to 0.15625
- dt_weight: bfloat16 [48, 1536], replicated, may hold values from -0.875 to 0.875
- dt_bias: float32 [1536], replicated, may hold values from -6.9 to -2.3
- a_log: float32 [16, 1536], replicated, may hold values from 0 to 2.77
- skip: float32 [1536], replicated, may hold values from 0.5 to 1.5
- out_weight: bfloat16 [1536, 768], replicated, may hold values from -0.4375 to 0.4375
- cotangent: bfloat16 [16, 256, 768], P('rows', 'seq'), may hold values from -6 to 6
Outputs:
- output: bfloat16 [16, 256, 768], P('rows', 'seq')
- grad_tokens: bfloat16 [16, 256, 768], P('rows', 'seq')
- grad_gain: float32 [768], replicated
- grad_in: float32 [768, 3072], replicated
- grad_conv: float32 [4, 1536], replicated
- grad_conv_bias: float32 [1536], replicated
- grad_x: float32 [80, 1536], replicated
- grad_dt: float32 [48, 1536], replicated
- grad_dt_bias: float32 [1536], replicated
- grad_a_log: float32 [16, 1536], replicated
- grad_skip: float32 [1536], replicated
- grad_out: float32 [1536, 768], replicated
Inputs may be any that keep to these rules, and one draw needn't show every extreme that they name: `marks`: in every row, one to three positions among 1 to 63 hold 1 (at least one), and zero to three among the last 64 positions; all other entries are 0.
All inputs are finite; a program needn't handle non-finite values.
Results may differ from a plain program's by a relative error of at most 0.012.
The roundings to bfloat16 on the way count: a program that leaves them out, or rounds other values in their place, can miss the bound.
Values may be sent and summed in bfloat16 or wider, within the bound.
A program may use at most 128 MiB of HBM per device.

v0:
```python
import jax
import jax.numpy as jnp
from jax import lax
from jax.experimental import pallas as pl
from jax.experimental.pallas import tpu as pltpu
from jax.sharding import PartitionSpec as P

f32 = jnp.float32
bf16 = jnp.bfloat16
EPS = 1e-05
LOG2E = 1.4426950408889634
LN2 = 0.6931471805599453
LANES = 128
STEP = 16
PLANE = 4
DEPTH = 4
TEAM = PLANE * DEPTH
MESH = pl.DeviceIdType.MESH
NN = (((1,), (0,)), ((), ()))
NT = (((1,), (1,)), ((), ()))
TN = (((0,), (0,)), ((), ()))


def mm(a, b, dims=NN):
    return lax.dot_general(a, b, dims, preferred_element_type=f32)


def lane_tiles(width, size):
    return [slice(j, j + size) for j in range(0, width, size)]


def body_kernel(
    tok, marks, gain, win, cw, cb, xw, dtw, dtb, alog, skip, wout, cot,
    out, gtok, gin, gout, small,
    win_i, win_g, wo, nfull, gfull, nh, gh, mk, mcol,
    inner, gate, dgated, act, dsilu, actl, ddec, u, ul, sig, dyf, dyl, du, s1, sq,
    pp, pq, pp2, pq2, hs, bt, ct, cbd, bbd, gbuf, qbuf, mc, mb,
    gt, dgl, dpl, dil, dconv, dn, dnr, outp, outr,
    fac, pf, pown, pb, zr, res, sm, smb, fs, zs, ress,
    ls, ss, rs,
):
    row, core = lax.axis_index("rows"), lax.axis_index("seq")
    other = 1 - core
    team = row - row % TEAM
    px, py, pz = row % 2, (row // 2) % 2, (row // PLANE) % DEPTH
    tl, d = tok.shape
    t = 2 * tl
    w = wo.shape[0]
    states = alog.shape[0]
    rank = dtw.shape[0]
    nproj = xw.shape[0]
    half = w // 2
    zrows = half // DEPTH
    chunks = t // STEP
    tiles = w // LANES
    mine = pl.multiple_of(core * tl, tl)
    theirs = pl.multiple_of(other * tl, tl)
    chan = pl.multiple_of(core * w, w)
    halves = lane_tiles(w, half)
    pending = []

    def plane_peer(s):
        x, y = s % 2, s // 2
        qx, qy = px + x - 2 * x * px, py + y - 2 * y * py
        return team + pz * PLANE + qy * 2 + qx, qx, qy

    def z_peer(s):
        return (pz + s) % DEPTH

    def send(k, src, dst, to_row, to_core):
        copy = pltpu.make_async_remote_copy(
            src_ref=src,
            dst_ref=dst,
            send_sem=ss.at[k],
            recv_sem=rs.at[k],
            device_id=(to_row, to_core),
            device_id_type=MESH,
        )
        copy.start()
        pending.append(copy)
        return copy

    def at_half(index):
        return pl.ds(pl.multiple_of(index * half, half), half)

    ids = iter(range(10_000))

    loads = [
        pltpu.make_async_copy(win.at[:, pl.ds(chan, w)], win_i, ls.at[0]),
        pltpu.make_async_copy(
            win.at[:, pl.ds(pl.multiple_of(2 * w + core * w, w), w)], win_g, ls.at[1]
        ),
        pltpu.make_async_copy(wout.at[pl.ds(chan, w), :], wo, ls.at[2]),
    ]
    for copy in loads:
        copy.start()

    gain_row = gain[...]
    unit = 2 * STEP

    def norm_block(b, carry):
        at = pl.multiple_of(b * unit, unit)
        rows = tok[pl.ds(at, unit), :].astype(f32)
        scale = lax.rsqrt(jnp.mean(rows * rows, axis=-1, keepdims=True) + EPS)
        nfull[pl.ds(mine + at, unit), :] = (rows * scale * gain_row).astype(bf16)
        gfull[pl.ds(mine + at, unit), :] = cot[pl.ds(at, unit), :]
        return carry

    lax.fori_loop(0, tl // unit, norm_block, 0)
    mk[:, pl.ds(mine, tl)] = jnp.broadcast_to(marks[...].astype(f32), (8, tl))

    barrier = pltpu.get_barrier_semaphore()
    partners = [(row, other)]
    partners += [(plane_peer(s)[0], core) for s in range(1, PLANE)]
    partners += [(team + z_peer(s) * PLANE + py * 2 + px, core) for s in range(1, DEPTH)]
    for partner in partners:
        pl.semaphore_signal(barrier, inc=1, device_id=partner, device_id_type=MESH)
    pl.semaphore_wait(barrier, len(partners))

    twin = []
    for ref in (nfull, gfull):
        part = ref.at[pl.ds(mine, tl), :]
        twin.append(send(next(ids), part, part, row, other))
    part = mk.at[:, pl.ds(mine, tl)]
    twin.append(send(next(ids), part, part, row, other))
    early = []
    for s in range(1, PLANE):
        peer, qx, qy = plane_peer(s)
        for full, dest in ((nfull, nh), (gfull, gh)):
            early.append(
                (
                    s,
                    dest,
                    send(
                        next(ids),
                        full.at[pl.ds(mine, tl), at_half(qy)],
                        dest.at[s - 1, pl.ds(mine, tl), :],
                        peer,
                        core,
                    ),
                )
            )

    inner[0:8, :] = jnp.zeros((8, w), f32)
    dconv[t : t + 8, :] = jnp.zeros((8, w), f32)
    mcol[t : t + 8, :] = jnp.zeros((8, LANES), f32)
    hs[0:states, :] = jnp.zeros((states, w), bf16)
    sm[...] = jnp.zeros(sm.shape, f32)

    for copy in loads:
        copy.wait()
    for copy in twin:
        copy.wait_recv()

    for sl in lane_tiles(w, 2 * LANES):
        inner[8 : 8 + t, sl] = mm(nfull[...], win_i[:, sl]).astype(bf16).astype(f32)

    lane = lax.broadcasted_iota(jnp.int32, (8, t), 1)
    mark = mk[...]
    keep = jnp.where(lane == 0, 0.0, 1.0 - mark)
    mask2 = keep * pltpu.roll(keep, 1, 1)
    mask3 = mask2 * pltpu.roll(keep, 2, 1)
    line = lax.broadcasted_iota(jnp.int32, (LANES, t), 0)

    def spread(v):
        return jnp.broadcast_to(v[0:1, :], (LANES, t))

    stacked = jnp.where(line == 0, spread(keep), 0.0)
    stacked = jnp.where(line == 1, spread(mask2), stacked)
    stacked = jnp.where(line == 2, spread(mask3), stacked)
    stacked = jnp.where(line == 3, spread(mark), stacked)
    mcol[0:t, :] = stacked.T

    cw_own = cw[:, pl.ds(chan, w)]
    cb_own = cb[:, pl.ds(chan, w)]
    taps = cw.shape[0]

    def conv_block(b, carry):
        at = pl.multiple_of(b * STEP, STEP)
        view = inner.at[pl.ds(at, STEP + 8)]
        masks = mcol[pl.ds(at, STEP), :]
        for sl in halves:
            total = cb_own[:, sl] + cw_own[taps - 1 : taps, sl] * view[8 : 8 + STEP, sl]
            for j in range(1, taps):
                tap = cw_own[taps - 1 - j : taps - j, sl]
                total = total + tap * view[8 - j : 8 - j + STEP, sl] * masks[:, j - 1 : j]
            sg = 1.0 / (1.0 + jnp.exp(-total))
            value = total * sg
            act[pl.ds(at, STEP), sl] = value
            actl[pl.ds(at, STEP), sl] = value.astype(bf16)
            dsilu[pl.ds(at, STEP), sl] = sg * (1.0 + total * (1.0 - sg))
        return carry

    lax.fori_loop(0, chunks, conv_block, 0)
    xw_own = xw[:, pl.ds(chan, w)]
    pp[:, 0:nproj] = mm(actl[...], xw_own, NT)
    proj_copy = send(next(ids), pp, pq, row, other)

    for sl in lane_tiles(w, 2 * LANES):
        gate[:, sl] = mm(nfull[...], win_g[:, sl])
        dgated[:, sl] = mm(gfull[...], wo[sl, :], NT)

    def dy_block(b, carry):
        at = pl.ds(pl.multiple_of(b * STEP, STEP), STEP)
        for sl in halves:
            g = gate[at, sl]
            low = (dgated[at, sl] * (g / (1.0 + jnp.exp(-g)))).astype(bf16)
            dyl[at, sl] = low
            dyf[at, sl] = low.astype(f32)
        return carry

    lax.fori_loop(0, chunks, dy_block, 0)

    relays = []
    for s, dest, copy in early:
        copy.wait_recv()
        part = dest.at[s - 1, pl.ds(mine, tl), :]
        relays.append(send(next(ids), part, part, row, other))

    proj_copy.wait_recv()
    proj = pp[...] + pq[...]
    turned = proj.T
    for k in range(chunks):
        cols = slice(k * STEP, (k + 1) * STEP)
        bt[k, :, 0:STEP] = turned[rank : rank + states, cols]
        ct[k, :, 0:STEP] = turned[rank + states : rank + 2 * states, cols]
    rank_low = proj[:, 0:rank].astype(bf16)
    rank_turned = turned[0:rank, :].astype(bf16)
    dtw_own = dtw[:, pl.ds(chan, w)]
    dtb_own = dtb[:, pl.ds(chan, w)]
    for sl in lane_tiles(w, 2 * LANES):
        sig[:, sl] = mm(rank_low, dtw_own[:, sl]) + dtb_own[:, sl]

    def delta_block(b, carry):
        at = pl.ds(pl.multiple_of(b * STEP, STEP), STEP)
        marked = mcol[at, :][:, 3:4] > 0.5
        for sl in halves:
            pre = sig[at, sl]
            e = jnp.exp(-jnp.abs(pre))
            one = 1.0 + e
            log1p = jnp.where(one == 1.0, e, jnp.log(one) * (e / (one - 1.0)))
            delta = jnp.maximum(pre, 0.0) + log1p
            sig[at, sl] = jnp.where(pre >= 0.0, 1.0, e) / one
            inflow = delta * act[at, sl]
            u[at, sl] = inflow
            ul[at, sl] = inflow.astype(bf16)
            s1[at, sl] = delta
            ddec[at, sl] = jnp.where(marked, 1e30, delta)
        return carry

    lax.fori_loop(0, chunks, delta_block, 0)

    span = STEP * states
    pick = (
        lax.broadcasted_iota(jnp.int32, (states, span), 0)
        == lax.broadcasted_iota(jnp.int32, (states, span), 1) % states
    ).astype(bf16)
    diag = (
        lax.broadcasted_iota(jnp.int32, (t, span), 0) % STEP
        == lax.broadcasted_iota(jnp.int32, (t, span), 1) // states
    )
    ones_diag = diag[0:STEP].astype(bf16)
    b_low = proj[:, rank : rank + states].astype(bf16)
    c_low = proj[:, rank + states : rank + 2 * states].astype(bf16)
    bbd[...] = jnp.where(diag, mm(b_low, pick), 0.0).astype(bf16)
    cbd[...] = jnp.where(diag, mm(c_low, pick), 0.0).astype(bf16)

    rates = [-jnp.exp(alog[:, pl.ds(chan + j * LANES, LANES)]) * LOG2E for j in range(tiles)]
    zeros = tuple(jnp.zeros((states, LANES), f32) for _ in range(tiles))

    def scan_chunk(k, state):
        base = pl.multiple_of(k * STEP, STEP)
        b_here = bt[k]
        dec, flow = ddec.at[pl.ds(base, STEP)], u.at[pl.ds(base, STEP)]
        state = list(state)
        for i in range(STEP):
            b_wide = jnp.broadcast_to(b_here[:, i : i + 1], (states, LANES))
            for j in range(tiles):
                sl = slice(j * LANES, (j + 1) * LANES)
                decay = jnp.exp2(dec[i : i + 1, sl] * rates[j])
                state[j] = decay * state[j] + flow[i : i + 1, sl] * b_wide
                hs[pl.ds(pl.multiple_of((base + i + 1) * states, states), states), sl] = state[
                    j
                ].astype(bf16)
        kept = hs[pl.ds(pl.multiple_of((base + 1) * states, states), span), :]
        du[pl.ds(base, STEP), :] = mm(cbd[pl.ds(base, STEP), :], kept)
        return tuple(state)

    lax.fori_loop(0, chunks, scan_chunk, zeros)

    skip_own = skip[:, pl.ds(chan, w)]

    def gated_block(b, carry):
        at = pl.ds(pl.multiple_of(b * STEP, STEP), STEP)
        for sl in halves:
            y = (du[at, sl] + skip_own[:, sl] * act[at, sl]).astype(bf16).astype(f32)
            g = gate[at, sl]
            sg = 1.0 / (1.0 + jnp.exp(-g))
            gt[at, sl] = (y * (g * sg)).astype(bf16)
            dgl[at, sl] = (dgated[at, sl] * y * (sg * (1.0 + g * (1.0 - sg)))).astype(bf16)
        return carry

    lax.fori_loop(0, chunks, gated_block, 0)

    def send_factors(n, source):
        copies = []
        for s in range(1, PLANE):
            peer, qx, qy = plane_peer(s)
            copies.append(
                send(next(ids), source.at[:, at_half(qx)], fac.at[n, s - 1], peer, core)
            )
        return copies

    fac_out = send_factors(0, gt)
    fac_gate = send_factors(1, dgl)

    for sl in lane_tiles(d, 2 * LANES):
        outp[:, sl] = mm(gt[...], wo[:, sl])
    out_copy = send(next(ids), outp.at[pl.ds(theirs, tl), :], outr, row, other)
    for sl in lane_tiles(d, 2 * LANES):
        dn[:, sl] = mm(dgl[...], win_g[sl, :], NT)

    def at_shard(n, z):
        first = px if n == 0 else py
        second = py if n == 0 else px
        return (
            pl.ds(pl.multiple_of(first * half + z * zrows, zrows), zrows),
            at_half(second),
        )

    def partial_sum(n, source, copies):
        for copy in copies:
            copy.wait_recv()
        for sl in lane_tiles(half, LANES):
            if n == 0:
                lefts = [source[:, at_half(px)][:, sl]] + [fac[0, s, :, sl] for s in range(PLANE - 1)]
                rights = [gfull[:, at_half(py)]] + [gh[s] for s in range(PLANE - 1)]
            else:
                lefts = [nfull[:, at_half(py)][:, sl]] + [nh[s, :, sl] for s in range(PLANE - 1)]
                rights = [source[:, at_half(px)]] + [fac[n, s] for s in range(PLANE - 1)]
            total = mm(lefts[0], rights[0], TN)
            for a, b in zip(lefts[1:], rights[1:]):
                total = total + mm(a, b, TN)
            pf[sl, :] = total
            pb[n, sl, :] = total.astype(bf16)
        pown[n] = pf[pl.ds(pl.multiple_of(pz * zrows, zrows), zrows), :]
        copies = []
        for s in range(1, DEPTH):
            to = z_peer(s)
            copies.append(
                send(
                    next(ids),
                    pb.at[n, pl.ds(pl.multiple_of(to * zrows, zrows), zrows), :],
                    zr.at[n, s - 1],
                    team + to * PLANE + py * 2 + px,
                    core,
                )
            )
        return copies

    def to_plane(n, z):
        rows, cols = at_shard(n, z)
        part = res.at[n, rows, cols]
        return [send(next(ids), part, part, plane_peer(s)[0], core) for s in range(1, PLANE)]

    def total_sum(n, copies):
        for copy in copies:
            copy.wait_recv()
        total = pown[n]
        for s in range(DEPTH - 1):
            total = total + zr[n, s].astype(f32)
        rows, cols = at_shard(n, pz)
        res[n, rows, cols] = total.astype(bf16)
        part = res.at[n, rows, cols]
        along = [
            send(next(ids), part, part, team + z_peer(s) * PLANE + py * 2 + px, core)
            for s in range(1, DEPTH)
        ]
        return along, to_plane(n, pz)

    def pass_on(n, along, across):
        for s in range(1, DEPTH):
            along[s - 1].wait_recv()
            across = across + to_plane(n, (pz + DEPTH - s) % DEPTH)
        return across

    def place_of(n):
        if n == 0:
            return gout.at[pl.ds(chan, w), :]
        return gin.at[:, pl.ds(pl.multiple_of((2 - n) * 2 * w + core * w, w), w)]

    locals_ = []

    def finish(n, across):
        for copy in across:
            copy.wait_recv()
        copy = pltpu.make_async_copy(res.at[n], place_of(n), ls.at[3 + n])
        copy.start()
        locals_.append(copy)
        return send(next(ids), res.at[n], place_of(n), row, other)

    def back_chunk(kk, carry):
        k = chunks - 1 - kk
        base = pl.multiple_of(k * STEP, STEP)
        c_here = ct[k]
        dec, dys = ddec.at[pl.ds(base, STEP)], dyf.at[pl.ds(base, STEP)]
        flow, acc = list(carry[0]), list(carry[1])
        for i in reversed(range(STEP)):
            c_wide = jnp.broadcast_to(c_here[:, i : i + 1], (states, LANES))
            line_at = slice(i * states, (i + 1) * states)
            for j in range(tiles):
                sl = slice(j * LANES, (j + 1) * LANES)
                rate = dec[i : i + 1, sl]
                g = c_wide * dys[i : i + 1, sl] + flow[j]
                gbuf[line_at, sl] = g.astype(bf16)
                flow[j] = g * jnp.exp2(rate * rates[j])
                before = hs[pl.ds(pl.multiple_of((base + i) * states, states), states), sl]
                q = flow[j] * before.astype(f32)
                acc[j] = acc[j] + q * rate
                qbuf[line_at, sl] = (q * rates[j]).astype(bf16)
        rows = pl.ds(base, STEP)
        kept = hs[pl.ds(pl.multiple_of((base + 1) * states, states), span), :]
        du[rows, :] = mm(bbd[rows, :], gbuf[...])
        sq[rows, :] = mm(ones_diag, qbuf[...])
        mc[rows, :] = mm(dyl[rows, :], kept, NT)
        mb[rows, :] = mm(ul[rows, :], gbuf[...], NT)
        return tuple(flow), tuple(acc)

    out_copy.wait_recv()

    def out_block(b, carry):
        at = pl.multiple_of(b * STEP, STEP)
        rows = pl.ds(at, STEP)
        total = outp[pl.ds(mine + at, STEP), :] + outr[rows, :]
        out[rows, :] = (tok[rows, :].astype(f32) + total).astype(bf16)
        return carry

    lax.fori_loop(0, tl // STEP, out_block, 0)

    marks_at = [chunks * p // 16 for p in (0, 4, 8, 11, 14, 16)]
    carry = (zeros, zeros)
    carry = lax.fori_loop(marks_at[0], marks_at[1], back_chunk, carry)
    for copy in relays:
        copy.wait_recv()
    z_out = partial_sum(0, gt, fac_out)
    carry = lax.fori_loop(marks_at[1], marks_at[2], back_chunk, carry)
    z_gate = partial_sum(1, dgl, fac_gate)
    carry = lax.fori_loop(marks_at[2], marks_at[3], back_chunk, carry)
    a_out = total_sum(0, z_out)
    carry = lax.fori_loop(marks_at[3], marks_at[4], back_chunk, carry)
    a_gate = total_sum(1, z_gate)
    c_out = pass_on(0, *a_out)
    carry = lax.fori_loop(marks_at[4], marks_at[5], back_chunk, carry)
    acc = carry[1]

    def fold(m):
        v = jnp.where(diag, m[...], 0.0)
        high = v.astype(bf16)
        rest = (v - high.astype(f32)).astype(bf16)
        return mm(high, pick, NT) + mm(rest, pick, NT)

    def dpre_block(b, carry):
        at = pl.ds(pl.multiple_of(b * STEP, STEP), STEP)
        sums, gains = [], []
        for n, sl in enumerate(halves):
            flow, value, dy = du[at, sl], act[at, sl], dyf[at, sl]
            dpre = (sq[at, sl] * LN2 + flow * value) * sig[at, sl]
            dpl[at, sl] = dpre.astype(bf16)
            du[at, sl] = flow * s1[at, sl] + skip_own[:, sl] * dy
            both = dy * value
            sums.append(carry[0][n] + dpre[0:8] + dpre[8:16])
            gains.append(carry[1][n] + both[0:8] + both[8:16])
        return tuple(sums), tuple(gains)

    none = tuple(jnp.zeros((8, half), f32) for _ in halves)
    sums, gains = lax.fori_loop(0, chunks, dpre_block, (none, none))
    first = nproj + rank + states
    line_conv, line_cb, line_dtb, line_skip, line_gain = (
        first,
        first + taps,
        first + taps + 1,
        first + taps + 2,
        first + taps + 3,
    )
    for n, sl in enumerate(halves):
        sm[line_dtb : line_dtb + 1, sl] = jnp.sum(sums[n], axis=0, keepdims=True)
        sm[line_skip : line_skip + 1, sl] = jnp.sum(gains[n], axis=0, keepdims=True)
    for j in range(tiles):
        sl = slice(j * LANES, (j + 1) * LANES)
        sm[nproj + rank : first, sl] = acc[j] * rates[j] * LN2

    pp2[:, 0:rank] = mm(dpl[...], dtw_own, NT)
    pp2[:, rank : rank + states] = fold(mb)
    pp2[:, rank + states : nproj] = fold(mc)
    dproj_copy = send(next(ids), pp2, pq2, row, other)
    for sl in lane_tiles(w, 2 * LANES):
        sm[nproj : nproj + rank, sl] = mm(rank_turned, dpl[:, sl])
    c_gate = pass_on(1, *a_gate)
    dproj_copy.wait_recv()
    dproj = pp2[...] + pq2[...]
    dproj_low = dproj[:, 0:nproj].astype(bf16)
    dproj_turned = dproj.T[0:nproj, :].astype(bf16)
    for sl in lane_tiles(w, 2 * LANES):
        sq[:, sl] = mm(dproj_low, xw_own[:, sl])

    def dconv_block(b, carry):
        at = pl.multiple_of(b * STEP, STEP)
        view = inner.at[pl.ds(at, STEP + 8)]
        rows = pl.ds(at, STEP)
        masks = mcol[rows, :]
        sums = [list(v) for v in carry]
        for n, sl in enumerate(halves):
            grad = (du[rows, sl] + sq[rows, sl]) * dsilu[rows, sl]
            dconv[rows, sl] = grad
            terms = [grad, grad * view[8 : 8 + STEP, sl]]
            for j in range(1, taps):
                terms.append(grad * masks[:, j - 1 : j] * view[8 - j : 8 - j + STEP, sl])
            for m, term in enumerate(terms):
                sums[m][n] = sums[m][n] + term[0:8] + term[8:16]
        return tuple(tuple(v) for v in sums)

    sums = lax.fori_loop(0, chunks, dconv_block, (none,) * (taps + 1))
    for n, sl in enumerate(halves):
        sm[line_cb : line_cb + 1, sl] = jnp.sum(sums[0][n], axis=0, keepdims=True)
        for j in range(taps):
            at = line_conv + taps - 1 - j
            sm[at : at + 1, sl] = jnp.sum(sums[1 + j][n], axis=0, keepdims=True)

    def dinner_block(b, carry):
        at = pl.multiple_of(b * STEP, STEP)
        view = dconv.at[pl.ds(at, STEP + 8)]
        masks = mcol.at[pl.ds(at, STEP + 8)]
        for sl in halves:
            total = cw_own[taps - 1 : taps, sl] * view[0:STEP, sl]
            for j in range(1, taps):
                tap = cw_own[taps - 1 - j : taps - j, sl]
                total = total + tap * view[j : j + STEP, sl] * masks[j : j + STEP, j - 1 : j]
            dil[pl.ds(at, STEP), sl] = total.astype(bf16)
        return carry

    lax.fori_loop(0, chunks, dinner_block, 0)
    fac_in = send_factors(2, dil)
    for sl in lane_tiles(d, 2 * LANES):
        dn[:, sl] = dn[:, sl] + mm(dil[...], win_i[sl, :], NT)
    dn_copy = send(next(ids), dn.at[pl.ds(theirs, tl), :], dnr, row, other)
    for sl in lane_tiles(w, 2 * LANES):
        sm[0:nproj, sl] = mm(dproj_turned, actl[:, sl])
    twin_out = finish(0, c_out)
    dn_copy.wait_recv()

    def norm_back(b, carry):
        at = pl.multiple_of(b * STEP, STEP)
        rows = pl.ds(at, STEP)
        values = tok[rows, :].astype(f32)
        scale = lax.rsqrt(jnp.mean(values * values, axis=-1, keepdims=True) + EPS)
        unit_rows = values * scale
        grad = dn[pl.ds(mine + at, STEP), :] + dnr[rows, :]
        inside = grad * gain_row
        mean = jnp.mean(inside * unit_rows, axis=-1, keepdims=True)
        both = grad * unit_rows
        gtok[rows, :] = (cot[rows, :].astype(f32) + scale * (inside - unit_rows * mean)).astype(bf16)
        return carry + both[0:8] + both[8:16]

    total = lax.fori_loop(0, tl // STEP, norm_back, jnp.zeros((8, d), f32))
    sm[line_gain : line_gain + 1, :] = jnp.sum(total, axis=0, keepdims=True)
    smb[...] = sm[...].astype(bf16)

    srows = smb.shape[0] // 2
    small_at = pl.ds(pl.multiple_of(py * srows, srows), srows)
    over_plane = []
    for s in range(1, PLANE):
        peer, qx, qy = plane_peer(s)
        over_plane.append(
            send(
                next(ids),
                smb.at[pl.ds(pl.multiple_of(qy * srows, srows), srows), at_half(qx)],
                fs.at[s - 1],
                peer,
                core,
            )
        )

    z_in = partial_sum(2, dil, fac_in)
    for copy in over_plane:
        copy.wait_recv()
    total = sm[small_at, at_half(px)]
    for s in range(PLANE - 1):
        total = total + fs[s].astype(f32)
    zs[pz] = total.astype(bf16)
    over_z = [
        send(next(ids), zs.at[pz], zs.at[pz], team + z_peer(s) * PLANE + py * 2 + px, core)
        for s in range(1, DEPTH)
    ]
    a_in = total_sum(2, z_in)
    for copy in over_z:
        copy.wait_recv()
    total = zs[0].astype(f32)
    for s in range(1, DEPTH):
        total = total + zs[s].astype(f32)
    ress[small_at, at_half(px)] = total.astype(bf16)
    part = ress.at[small_at, at_half(px)]
    small_across = [send(next(ids), part, part, plane_peer(s)[0], core) for s in range(1, PLANE)]
    twin_gate = finish(1, c_gate)
    c_in = pass_on(2, *a_in)
    for copy in small_across:
        copy.wait_recv()
    small_copy = pltpu.make_async_copy(ress, small.at[:, pl.ds(chan, w)], ls.at[6])
    small_copy.start()
    locals_.append(small_copy)
    twin_small = send(next(ids), ress, small.at[:, pl.ds(chan, w)], row, other)
    twin_in = finish(2, c_in)
    for copy in (twin_out, twin_gate, twin_small, twin_in):
        copy.wait_recv()
    for copy in locals_:
        copy.wait()
    for copy in pending:
        copy.wait_send()


def wide_kernel(gin, gout, small, gin_f, gout_f, *rows):
    gin_f[...] = gin[...].astype(f32)
    gout_f[...] = gout[...].astype(f32)

    @pl.when(pl.program_id(0) == 0)
    def _():
        whole = small[...].astype(f32)
        first = 0
        for ref in rows[:-1]:
            count = ref.shape[0]
            ref[...] = whole[first : first + count, :]
            first += count
        width = rows[-1].shape[1]
        line = whole[first : first + 1, :]
        rows[-1][...] = line[:, 0:width] + line[:, width : 2 * width]


def local(
    tokens, marks, norm_gain, in_weight, conv_weight, conv_bias, x_weight, dt_weight,
    dt_bias, a_log, skip, out_weight, cotangent,
):
    tl, d = tokens.shape[1:]
    e = out_weight.shape[0]
    w = e // lax.axis_size("seq")
    t = tl * lax.axis_size("seq")
    states, rank, nproj, taps = a_log.shape[0], dt_weight.shape[0], x_weight.shape[0], conv_weight.shape[0]
    half, chunks, span = w // 2, t // STEP, STEP * states
    zrows = half // DEPTH
    lines = -(-(nproj + rank + states + taps + 4) // 32) * 32
    vmem = pl.BlockSpec(memory_space=pltpu.VMEM)
    anywhere = pl.BlockSpec(memory_space=pl.ANY)
    wide = pltpu.VMEM((t, w), f32)
    low = pltpu.VMEM((t, w), bf16)
    scratch = [
        pltpu.VMEM((d, w), bf16), pltpu.VMEM((d, w), bf16), pltpu.VMEM((w, d), bf16),
        pltpu.VMEM((t, d), bf16), pltpu.VMEM((t, d), bf16),
        pltpu.VMEM((PLANE - 1, t, half), bf16), pltpu.VMEM((PLANE - 1, t, half), bf16),
        pltpu.VMEM((8, t), f32), pltpu.VMEM((t + 8, LANES), f32),
        pltpu.VMEM((t + 8, w), f32), wide, wide, wide, wide, low, wide, wide, low, wide, wide, low,
        wide, wide, wide,
        pltpu.VMEM((t, LANES), f32), pltpu.VMEM((t, LANES), f32),
        pltpu.VMEM((t, LANES), f32), pltpu.VMEM((t, LANES), f32),
        pltpu.VMEM(((t + 1) * states, w), bf16),
        pltpu.VMEM((chunks, states, LANES), f32), pltpu.VMEM((chunks, states, LANES), f32),
        pltpu.VMEM((t, span), bf16), pltpu.VMEM((t, span), bf16),
        pltpu.VMEM((span, w), bf16), pltpu.VMEM((span, w), bf16),
        pltpu.VMEM((t, span), f32), pltpu.VMEM((t, span), f32),
        low, low, low, low, pltpu.VMEM((t + 8, w), f32),
        pltpu.VMEM((t, d), f32), pltpu.VMEM((tl, d), f32),
        pltpu.VMEM((t, d), f32), pltpu.VMEM((tl, d), f32),
        pltpu.VMEM((3, PLANE - 1, t, half), bf16), pltpu.VMEM((half, half), f32),
        pltpu.VMEM((3, zrows, half), f32), pltpu.VMEM((3, half, half), bf16),
        pltpu.VMEM((3, DEPTH - 1, zrows, half), bf16), pltpu.VMEM((3, w, d), bf16),
        pltpu.VMEM((lines, w), f32), pltpu.VMEM((lines, w), bf16),
        pltpu.VMEM((PLANE - 1, lines // 2, half), bf16), pltpu.VMEM((DEPTH, lines // 2, half), bf16),
        pltpu.VMEM((lines, w), bf16),
        pltpu.SemaphoreType.DMA((8,)),
        pltpu.SemaphoreType.DMA((112,)), pltpu.SemaphoreType.DMA((112,)),
    ]
    output, grad_tokens, gin, gout, small = pl.pallas_call(
        body_kernel,
        out_shape=[
            jax.ShapeDtypeStruct((tl, d), bf16),
            jax.ShapeDtypeStruct((tl, d), bf16),
            jax.ShapeDtypeStruct((d, 2 * e), bf16),
            jax.ShapeDtypeStruct((e, d), bf16),
            jax.ShapeDtypeStruct((lines, e), bf16),
        ],
        in_specs=[vmem, vmem, vmem, anywhere] + [vmem] * 7 + [anywhere, vmem],
        out_specs=[vmem, vmem, anywhere, anywhere, anywhere],
        scratch_shapes=scratch,
        compiler_params=pltpu.CompilerParams(
            collective_id=0, has_side_effects=True, vmem_limit_bytes=60 * 2**20
        ),
        name="block",
    )(
        tokens.reshape(tl, d), marks.reshape(1, tl), norm_gain.reshape(1, d), in_weight, conv_weight,
        conv_bias.reshape(1, e), x_weight, dt_weight, dt_bias.reshape(1, e), a_log,
        skip.reshape(1, e), out_weight, cotangent.reshape(tl, d),
    )

    steps = 8
    shapes = [(nproj, e), (rank, e), (states, e), (taps, e), (1, e), (1, e), (1, e), (1, d)]
    once = [pl.BlockSpec(s, lambda i: (0, 0)) for s in shapes]
    gin_spec = pl.BlockSpec((d // steps, 2 * e), lambda i: (i, 0))
    gout_spec = pl.BlockSpec((e // steps, d), lambda i: (i, 0))
    grads = pl.pallas_call(
        wide_kernel,
        grid=(steps,),
        out_shape=[jax.ShapeDtypeStruct(s, f32) for s in [(d, 2 * e), (e, d)] + shapes],
        in_specs=[gin_spec, gout_spec, pl.BlockSpec((lines, e), lambda i: (0, 0))],
        out_specs=[gin_spec, gout_spec] + once,
        compiler_params=pltpu.CompilerParams(vmem_limit_bytes=32 * 2**20),
        name="widen",
    )(gin, gout, small)
    rows = lax.axis_size("rows")
    if rows > TEAM:
        grads = [v * (1.0 / TEAM) for v in lax.psum(grads, "rows")]
    grad_in, grad_out, grad_x, grad_dt, grad_log, grad_conv, g_cb, g_dtb, g_skip, g_gain = grads
    return (
        output[None], grad_tokens[None], g_gain.reshape(d), grad_in, grad_conv, g_cb.reshape(e), grad_x,
        grad_dt, g_dtb.reshape(e), grad_log, g_skip.reshape(e), grad_out,
    )


def solution(mesh):
    split = P("rows", "seq", None)
    whole = P()
    in_specs = (split, P("rows", "seq")) + (whole,) * 10 + (split,)
    out_specs = (split, split) + (whole,) * 10
    return jax.shard_map(local, mesh=mesh, in_specs=in_specs, out_specs=out_specs, check_vma=False)
```

profile of v0, /device:TPU:1, one launch (start us, length us, event | category | flops | bytes accessed | tf_op | source)
XLA Modules:
  0.0 135.6 jit_solution(11437671977667178804)
XLA Ops:
  0.6 1.3 reshape.55.gain
  1.9 1.3 reshape.56.cb
  3.2 1.3 reshape.57.dtb
  4.5 1.3 reshape.58.skip
  5.8 114.9 %block.1 = (bf16[128,768]{1,0:T(8,128)(2,1)}, bf16[128,768]{1,0:T(8,128)(2,1)}, bf16[768,3072]{1,0:T(8,128)(2,1)}, bf16[1536,768]{1,0:T(8,128)(2,1)}, bf16[160,1536]{1,0:T(8,128)(2,1)}) custom-call(bf16[128,768]{1,0:T(8,128)(2,1)} %bitcast.6, s32[1,128]{1,0:T(1,128)} %marks.1, f32[1,768]{1,0:T(1,128)} %reshape.55.gain, bf16[768,3072]{1,0:T(8,128)(2,1)} %win.1, ...), custom_call_target="tpu_custom_call" | custom-call | tf_op jit(solution)/shard_map/block/pallas_call | solution.py:679
  120.7 0.0 copy-start
  120.7 2.3 %copy-done = bf16[768,3072]{1,0:T(8,128)(2,1)S(1)} copy-done((bf16[768,3072]{1,0:T(8,128)(2,1)S(1)}, bf16[768,3072]{1,0:T(8,128)(2,1)}, u32[]{:S(2)}) %copy-start) | copy-done | bytes 4718616
  123.0 0.0 copy-start.1
  123.0 1.7 %copy-done.1 = bf16[1536,768]{1,0:T(8,128)(2,1)S(1)} copy-done((bf16[1536,768]{1,0:T(8,128)(2,1)S(1)}, bf16[1536,768]{1,0:T(8,128)(2,1)}, u32[]{:S(2)}) %copy-start.1) | copy-done | bytes 2359320
  124.7 0.0 copy-start.2
  124.7 1.0 copy-done.2
  125.7 0.0 copy-start.4
  125.7 0.0 copy-start.3
  125.7 6.1 %widen.1 = (f32[768,3072]{1,0:T(8,128)}, f32[1536,768]{1,0:T(8,128)}, f32[80,1536]{1,0:T(8,128)}, f32[48,1536]{1,0:T(8,128)}, f32[16,1536]{1,0:T(8,128)}, /*inde...) custom-call(bf16[768,3072]{1,0:T(8,128)(2,1)S(1)} %copy-done, ...), custom_call_target="tpu_custom_call" | custom-call | tf_op jit(solution)/shard_map/widen/pallas_call | solution.py:706
  131.8 0.6 reduce
  132.4 0.6 reduce.1
  133.1 0.6 reduce.2
  133.7 0.6 reduce.3
  134.3 0.0 copy-done.4
  134.3 0.7 copy.27
  135.0 0.0 copy-done.3
  135.0 0.7 copy.28
Async XLA Ops:
  120.7 2.3 %copy-start = (bf16[768,3072]{1,0:T(8,128)(2,1)S(1)}, bf16[768,3072]{1,0:T(8,128)(2,1)}, u32[]{:S(2)}) copy-start(bf16[768,3072]{1,0:T(8,128)(2,1)} %get-tuple-element.29.gin) | copy-start | bytes 14155780
  123.0 1.7 %copy-start.1 = (bf16[1536,768]{1,0:T(8,128)(2,1)S(1)}, bf16[1536,768]{1,0:T(8,128)(2,1)}, u32[]{:S(2)}) copy-start(bf16[1536,768]{1,0:T(8,128)(2,1)} %get-tuple-element.30.gout) | copy-start | bytes 7077892
  124.7 1.0 copy-start.2
  125.7 8.6 %copy-start.4 = (bf16[128,768]{1,0:T(8,128)(2,1)S(1)}, bf16[128,768]{1,0:T(8,128)(2,1)}, u32[]{:S(2)}) copy-start(bf16[128,768]{1,0:T(8,128)(2,1)} %get-tuple-element.27) | copy-start | bytes 589828
  125.7 9.2 %copy-start.3 = (bf16[128,768]{1,0:T(8,128)(2,1)S(1)}, bf16[128,768]{1,0:T(8,128)(2,1)}, u32[]{:S(2)}) copy-start(bf16[128,768]{1,0:T(8,128)(2,1)} %get-tuple-element.28) | copy-start | bytes 589828
where the time goes:
time: 136 us
  Pallas kernels  121 us (89%)
  local copies, waits for them, and re-layouts  11.5 us (8%)
  other arithmetic  2.46 us (2%)
    pallas_call x1, Pallas kernels, local(): pl.pallas_call(body_kernel, out_shape=[jax.ShapeDtypeStruct((tl, d), bf16...  115 us
    unnamed x12, local copies, waits for them, and re-layouts  6.39 us
    pallas_call x1, Pallas kernels, local(): pl.pallas_call(wide_kernel, grid=(steps,), out_shape=[jax.ShapeDtypeStruc...  6.09 us

commit v1 on v0

v1 whole, which is shorter than its diff:
```python
import functools

import jax
import jax.numpy as jnp
from jax import lax
from jax.experimental import pallas as pl
from jax.experimental.pallas import tpu as pltpu
from jax.sharding import PartitionSpec as P

f32 = jnp.float32
bf16 = jnp.bfloat16
EPS = 1e-05
LANES = 128
STEP = 16
PLANE = 4
DEPTH = 4
TEAM = PLANE * DEPTH
MESH = pl.DeviceIdType.MESH
NN = (((1,), (0,)), ((), ()))
NT = (((1,), (1,)), ((), ()))


def mm(a, b, dims=NN):
    return lax.dot_general(a, b, dims, preferred_element_type=f32)


def lane_tiles(width, size):
    return [slice(j, j + size) for j in range(0, width, size)]


def body_kernel(
    tok, marks, gain, win, cw, cb, xw, dtw, dtb, alog, skip, wout, cot,
    out, gtok, gin, gout, small,
    win_i, win_g, wo, ng, ngh, mk, mcol, lines,
    inner, gate, dgated, act, dsilu, actl, ddec, u, sig, dyf, du, s1, sq,
    pp, pq, pp2, pq2, tsc, even, odd, bt, ct, cbd, bbd, ga, gb, qa, qb, ba, bb, ca, cc, dbt, dct,
    gt, dgl, dpl, dil, turn, dconv, dn, dnr, outp, outr,
    fac, pw, pown, pb, zr, res, sm, smb, smf, sfac, szr, sres, sown, sfin,
    ls, ss, rs,
):
    row, core = lax.axis_index("rows"), lax.axis_index("seq")
    other = 1 - core
    team = row - row % TEAM
    px, py, pz = row % 2, (row // 2) % 2, (row // PLANE) % DEPTH
    tl, d = tok.shape
    t = 2 * tl
    w = wo.shape[0]
    states = alog.shape[0]
    rank = dtw.shape[0]
    nproj = xw.shape[0]
    half = w // 2
    quarter = w // PLANE
    zrows = quarter // DEPTH
    place = row % PLANE
    chunks = t // STEP
    tiles = w // LANES
    mine = pl.multiple_of(core * tl, tl)
    theirs = pl.multiple_of(other * tl, tl)
    chan = pl.multiple_of(core * w, w)
    halves = lane_tiles(w, half)
    pending = []

    def plane_place(s):
        x, y = s % 2, s // 2
        return (py + y - 2 * y * py) * 2 + px + x - 2 * x * px

    def plane_row(s):
        return team + pz * PLANE + plane_place(s)

    def z_place(s):
        return (pz + s) % DEPTH

    def z_row(s):
        return team + z_place(s) * PLANE + place

    def send(k, src, dst, to_row, to_core):
        copy = pltpu.make_async_remote_copy(
            src_ref=src,
            dst_ref=dst,
            send_sem=ss.at[k],
            recv_sem=rs.at[k],
            device_id=(to_row, to_core),
            device_id_type=MESH,
        )
        copy.start()
        pending.append(copy)
        return copy

    def block(index, size):
        return pl.ds(pl.multiple_of(index * size, size), size)

    ids = iter(range(10_000))

    loads = [
        pltpu.make_async_copy(win.at[:, pl.ds(chan, w)], win_i, ls.at[0]),
        pltpu.make_async_copy(
            win.at[:, pl.ds(pl.multiple_of(2 * w + core * w, w), w)], win_g, ls.at[1]
        ),
        pltpu.make_async_copy(wout.at[pl.ds(chan, w), :], wo, ls.at[2]),
    ]
    for copy in loads:
        copy.start()

    for n, ref in enumerate((gain, cb, dtb, skip)):
        count = ref.shape[0]
        lines[n : n + 1, 0:count] = ref[...].reshape(1, count)
    gain_row = lines[0:1, 0:d]
    unit = 2 * STEP

    def norm_block(b, carry):
        at = pl.multiple_of(b * unit, unit)
        rows = tok[pl.ds(at, unit), :].astype(f32)
        scale = lax.rsqrt(jnp.mean(rows * rows, axis=-1, keepdims=True) + EPS)
        ng[0, pl.ds(mine + at, unit), :] = (rows * scale * gain_row).astype(bf16)
        ng[1, pl.ds(mine + at, unit), :] = cot[pl.ds(at, unit), :]
        return carry

    lax.fori_loop(0, tl // unit, norm_block, 0)
    mk[:, pl.ds(mine, tl)] = jnp.broadcast_to(marks[...].astype(f32), (8, tl))

    barrier = pltpu.get_barrier_semaphore()
    partners = [(row, other)]
    partners += [(plane_row(s), core) for s in range(1, PLANE)]
    partners += [(z_row(s), core) for s in range(1, DEPTH)]
    for partner in partners:
        pl.semaphore_signal(barrier, inc=1, device_id=partner, device_id_type=MESH)
    pl.semaphore_wait(barrier, len(partners))

    own_rows = ng.at[:, pl.ds(mine, tl), :]
    twin = [send(next(ids), own_rows, own_rows, row, other)]
    part = mk.at[:, pl.ds(mine, tl)]
    twin.append(send(next(ids), part, part, row, other))
    early = [
        send(next(ids), own_rows, ngh.at[s - 1, :, pl.ds(mine, tl), :], plane_row(s), core)
        for s in (1, 2)
    ]

    inner[0:8, :] = jnp.zeros((8, w), f32)
    dconv[t : t + 8, :] = jnp.zeros((8, w), f32)
    mcol[t : t + 8, :] = jnp.zeros((8, LANES), f32)
    odd[0:states, :] = jnp.zeros((states, w), bf16)
    tsc[...] = jnp.zeros(tsc.shape, f32)
    smb[...] = jnp.zeros(smb.shape, bf16)
    for ref in (ga, qa, ba, ca):
        ref[...] = jnp.zeros(ref.shape, bf16)
    sm[...] = jnp.zeros(sm.shape, f32)

    for copy in loads:
        copy.wait()
    for copy in twin:
        copy.wait_recv()

    for sl in lane_tiles(w, 2 * LANES):
        inner[8 : 8 + t, sl] = mm(ng[0], win_i[:, sl]).astype(bf16).astype(f32)

    lane = lax.broadcasted_iota(jnp.int32, (8, t), 1)
    mark = mk[...]
    keep = jnp.where(lane == 0, 0.0, 1.0 - mark)
    mask2 = keep * pltpu.roll(keep, 1, 1)
    mask3 = mask2 * pltpu.roll(keep, 2, 1)
    line = lax.broadcasted_iota(jnp.int32, (LANES, t), 0)

    def spread(v):
        return jnp.broadcast_to(v[0:1, :], (LANES, t))

    stacked = jnp.where(line == 0, spread(keep), 0.0)
    stacked = jnp.where(line == 1, spread(mask2), stacked)
    stacked = jnp.where(line == 2, spread(mask3), stacked)
    stacked = jnp.where(line == 3, spread(mark), stacked)
    mcol[0:t, :] = stacked.T

    cw_own = cw[:, pl.ds(chan, w)]
    cb_own = lines[1:2, pl.ds(chan, w)]
    taps = cw.shape[0]

    def conv_block(b, carry):
        at = pl.multiple_of(b * STEP, STEP)
        view = inner.at[pl.ds(at, STEP + 8)]
        masks = mcol[pl.ds(at, STEP), :]
        for sl in halves:
            total = cb_own[:, sl] + cw_own[taps - 1 : taps, sl] * view[8 : 8 + STEP, sl]
            for j in range(1, taps):
                tap = cw_own[taps - 1 - j : taps - j, sl]
                total = total + tap * view[8 - j : 8 - j + STEP, sl] * masks[:, j - 1 : j]
            sg = 1.0 / (1.0 + jnp.exp(-total))
            value = total * sg
            act[pl.ds(at, STEP), sl] = value
            actl[pl.ds(at, STEP), sl] = value.astype(bf16)
            dsilu[pl.ds(at, STEP), sl] = sg * (1.0 + total * (1.0 - sg))
        return carry

    lax.fori_loop(0, chunks, conv_block, 0)
    xw_own = xw[:, pl.ds(chan, w)]
    pp[:, 0:nproj] = mm(actl[...], xw_own, NT)
    proj_copy = send(next(ids), pp, pq, row, other)

    for sl in lane_tiles(w, 2 * LANES):
        gate[:, sl] = mm(ng[0], win_g[:, sl])
        dgated[:, sl] = mm(ng[1], wo[sl, :], NT)

    def dy_block(b, carry):
        at = pl.ds(pl.multiple_of(b * STEP, STEP), STEP)
        for sl in halves:
            g = gate[at, sl]
            low = (dgated[at, sl] * (g / (1.0 + jnp.exp(-g)))).astype(bf16)
            dyf[at, sl] = low.astype(f32)
        return carry

    lax.fori_loop(0, chunks, dy_block, 0)

    across, relays = [], []
    for s in (1, 2):
        early[s - 1].wait_recv()
        piece = pl.ds(pl.multiple_of(mine + (s - 1) * (tl // 2), tl // 2), tl // 2)
        across.append(
            send(next(ids), ngh.at[s - 1, :, piece, :], ngh.at[2, :, piece, :], plane_row(3 - s), core)
        )
        part = ngh.at[s - 1, :, pl.ds(mine, tl), :]
        relays.append(send(next(ids), part, part, row, other))

    proj_copy.wait_recv()
    proj = pp[...] + pq[...]
    turned = proj.T
    for k in range(chunks):
        cols = slice(k * STEP, (k + 1) * STEP)
        bt[k, :, 0:STEP] = turned[rank : rank + states, cols]
        ct[k, :, 0:STEP] = turned[rank + states : rank + 2 * states, cols]
    rank_low = proj[:, 0:rank].astype(bf16)
    rank_turned = turned[0:rank, :].astype(bf16)
    dtw_own = dtw[:, pl.ds(chan, w)]
    dtb_own = lines[2:3, pl.ds(chan, w)]
    for sl in lane_tiles(w, 2 * LANES):
        sig[:, sl] = mm(rank_low, dtw_own[:, sl]) + dtb_own[:, sl]

    def delta_block(b, carry):
        at = pl.ds(pl.multiple_of(b * STEP, STEP), STEP)
        marked = mcol[at, :][:, 3:4] > 0.5
        for sl in halves:
            pre = sig[at, sl]
            e = jnp.exp(-jnp.abs(pre))
            one = 1.0 + e
            log1p = jnp.where(one == 1.0, e, jnp.log(one) * (e / (one - 1.0)))
            delta = jnp.maximum(pre, 0.0) + log1p
            sig[at, sl] = jnp.where(pre >= 0.0, 1.0, e) / one
            inflow = delta * act[at, sl]
            u[at, sl] = inflow
            s1[at, sl] = delta
            ddec[at, sl] = jnp.where(marked, 1e30, delta)
        return carry

    lax.fori_loop(0, chunks, delta_block, 0)

    span = STEP * states
    pick = (
        lax.broadcasted_iota(jnp.int32, (states, span), 0)
        == lax.broadcasted_iota(jnp.int32, (states, span), 1) % states
    ).astype(bf16)
    diag = (
        lax.broadcasted_iota(jnp.int32, (t, span), 0) % STEP
        == lax.broadcasted_iota(jnp.int32, (t, span), 1) // states
    )
    ones_diag = diag[0:STEP].astype(bf16)
    b_low = proj[:, rank : rank + states].astype(bf16)
    c_low = proj[:, rank + states : rank + 2 * states].astype(bf16)
    bbd[...] = jnp.where(diag, mm(b_low, pick), 0.0).astype(bf16)
    cbd[...] = jnp.where(diag, mm(c_low, pick), 0.0).astype(bf16)

    rates = [-jnp.exp(alog[:, pl.ds(chan + j * LANES, LANES)]) for j in range(tiles)]
    zeros = tuple(jnp.zeros((states, LANES), f32) for _ in range(tiles))
    tile = [slice(j * LANES, (j + 1) * LANES) for j in range(tiles)]

    def even_at(m):
        return pl.multiple_of(m * span, span)

    def odd_at(m):
        return pl.multiple_of(states + m * span, states)

    def state_block(ref, first, i):
        return ref.at[pl.ds(pl.multiple_of(first + i * states, states), states)]

    def scan_chunk(k, state, kept, first):
        rows = pl.ds(pl.multiple_of(k * STEP, STEP), STEP)
        b_here, dec, flow = bt[k], ddec.at[rows], u.at[rows]
        state = list(state)
        for i in range(STEP):
            b_wide = jnp.broadcast_to(b_here[:, i : i + 1], (states, LANES))
            dest = state_block(kept, first, i)
            for j, sl in enumerate(tile):
                decay = jnp.exp(dec[i : i + 1, sl] * rates[j])
                state[j] = decay * state[j] + flow[i : i + 1, sl] * b_wide
                dest[:, sl] = state[j].astype(bf16)
        return state

    def read_chunk(k, kept, first):
        rows = pl.ds(pl.multiple_of(k * STEP, STEP), STEP)
        du[rows, :] = mm(cbd[rows, :], kept[pl.ds(pl.multiple_of(first, states), span), :])

    def scan_pair(m, state):
        read_chunk(jnp.maximum(2 * m - 1, 0), odd, odd_at(jnp.maximum(m - 1, 0)))
        state = scan_chunk(2 * m, state, even, even_at(m))
        read_chunk(2 * m, even, even_at(m))
        return tuple(scan_chunk(2 * m + 1, state, odd, odd_at(m)))

    pairs = chunks // 2
    odd[pl.ds(states, span), :] = jnp.zeros((span, w), bf16)
    final = lax.fori_loop(0, pairs, scan_pair, zeros)
    read_chunk(chunks - 1, odd, odd_at(pairs - 1))

    skip_own = lines[3:4, pl.ds(chan, w)]

    def gated_block(b, carry):
        at = pl.ds(pl.multiple_of(b * STEP, STEP), STEP)
        for sl in halves:
            y = (du[at, sl] + skip_own[:, sl] * act[at, sl]).astype(bf16).astype(f32)
            g = gate[at, sl]
            sg = 1.0 / (1.0 + jnp.exp(-g))
            gt[at, sl] = (y * (g * sg)).astype(bf16)
            dgl[at, sl] = (dgated[at, sl] * y * (sg * (1.0 + g * (1.0 - sg)))).astype(bf16)
        return carry

    lax.fori_loop(0, chunks, gated_block, 0)

    def send_factors(n, source):
        for sl in tile:
            turn[n, sl, :] = source[:, sl].T
        return [
            send(
                next(ids),
                turn.at[n, block(plane_place(s), quarter), :],
                fac.at[n, s - 1],
                plane_row(s),
                core,
            )
            for s in range(1, PLANE)
        ]

    def partial_sum(n, copies):
        for copy in copies:
            copy.wait_recv()
        kind = 1 if n == 0 else 0
        lefts = [turn[n, block(place, quarter), :]] + [fac[n, s] for s in range(PLANE - 1)]
        for sl in lane_tiles(d, 2 * LANES):
            total = mm(lefts[0], ng[kind, :, sl])
            for s in range(PLANE - 1):
                total = total + mm(lefts[s + 1], ngh[s, kind, :, sl])
            pw[:, sl] = total
            pb[n, :, sl] = total.astype(bf16)
        pown[n] = pw[block(pz, zrows), :]
        return [
            send(next(ids), pb.at[n, block(z_place(s), zrows), :], zr.at[n, s - 1], z_row(s), core)
            for s in range(1, DEPTH)
        ]

    def shard(n, where, z):
        return res.at[n, pl.ds(pl.multiple_of(where * quarter + z * zrows, zrows), zrows), :]

    def to_neighbours(part):
        return [send(next(ids), part, part, plane_row(s), core) for s in (1, 2)]

    def total_sum(n, copies):
        for copy in copies:
            copy.wait_recv()
        total = pown[n]
        for s in range(DEPTH - 1):
            total = total + zr[n, s].astype(f32)
        part = shard(n, place, pz)
        part[...] = total.astype(bf16)
        along = [send(next(ids), part, part, z_row(s), core) for s in range(1, DEPTH)]
        return {"n": n, "along": along, "near": [to_neighbours(part)], "far": []}

    def pass_on(state, s):
        state["along"][s - 1].wait_recv()
        part = shard(state["n"], place, (pz + DEPTH - s) % DEPTH)
        state["near"].append(to_neighbours(part))

    def pass_across(state, s):
        for q in (1, 2):
            state["near"][s][q - 1].wait_recv()
        q = 1 + s % 2
        part = shard(state["n"], plane_place(q), (pz + DEPTH - s) % DEPTH)
        state["far"].append(send(next(ids), part, part, plane_row(3 - q), core))

    def place_of(n):
        if n == 0:
            return gout.at[pl.ds(chan, w), :]
        return gin.at[pl.ds(pl.multiple_of((2 - n) * 2 * w + core * w, w), w), :]

    locals_ = []

    def finish(state):
        n = state["n"]
        for copy in state["far"]:
            copy.wait_recv()
        copy = pltpu.make_async_copy(res.at[n], place_of(n), ls.at[3 + n])
        copy.start()
        locals_.append(copy)
        return send(next(ids), res.at[n], place_of(n), row, other)

    fac_out = send_factors(0, gt)
    fac_gate = send_factors(1, dgl)
    for s in (1, 2):
        across[s - 1].wait_recv()
        piece = pl.ds(pl.multiple_of(mine + (s - 1) * (tl // 2), tl // 2), tl // 2)
        part = ngh.at[2, :, piece, :]
        relays.append(send(next(ids), part, part, row, other))

    for sl in lane_tiles(d, 2 * LANES):
        outp[:, sl] = mm(gt[...], wo[:, sl])
    out_copy = send(next(ids), outp.at[pl.ds(theirs, tl), :], outr, row, other)
    for sl in lane_tiles(d, 2 * LANES):
        dn[:, sl] = mm(dgl[...], win_g[sl, :], NT)

    def back_chunk(k, carry, kept, first, before, last, gbuf, qbuf, bbuf, cbuf):
        base = pl.multiple_of(k * STEP, STEP)
        rows = pl.ds(base, STEP)
        c_here, dec, dys, inflow = ct[k], ddec.at[rows], dyf.at[rows], u.at[rows]
        dys_before = dyf.at[pl.ds(pl.multiple_of(jnp.maximum(base - STEP, 0), STEP), STEP)]
        flow, acc = list(carry[0]), list(carry[1])
        for i in reversed(range(STEP)):
            c_wide = jnp.broadcast_to(c_here[:, i : i + 1], (states, LANES))
            at = slice(i * states, (i + 1) * states)
            old = state_block(kept, first, i - 1) if i else state_block(before, last, 0)
            dy_old = dys_before[STEP - 1 : STEP, :] if i == 0 else dys[i - 1 : i, :]
            for_b = for_c = None
            for j, sl in enumerate(tile):
                rate = dec[i : i + 1, sl]
                g = c_wide * dys[i : i + 1, sl] + flow[j]
                gbuf[at, sl] = g.astype(bf16)
                flow[j] = g * jnp.exp(rate * rates[j])
                h_old = old[:, sl].astype(f32)
                q = flow[j] * h_old
                acc[j] = acc[j] + q * rate
                qbuf[at, sl] = (q * rates[j]).astype(bf16)
                term_b, term_c = g * inflow[i : i + 1, sl], h_old * dy_old[:, sl]
                for_b = term_b if for_b is None else for_b + term_b
                for_c = term_c if for_c is None else for_c + term_c
            bbuf[at, :] = for_b.astype(bf16)
            cbuf[at, :] = for_c.astype(bf16)
        return flow, acc

    lane_of = lax.broadcasted_iota(jnp.int32, (states, LANES), 1)
    ones = jnp.ones((LANES, LANES), bf16)

    def back_sums(k, gbuf, qbuf, bbuf, cbuf):
        rows = pl.ds(pl.multiple_of(k * STEP, STEP), STEP)
        for parts, dest in ((bbuf, dbt), (cbuf, dct)):
            summed = mm(parts[...], ones)
            value = jnp.zeros((states, LANES), f32)
            for i in range(STEP):
                value = jnp.where(lane_of == i, summed[i * states : (i + 1) * states, :], value)
            dest[k] = value
        du[rows, :] = mm(bbd[rows, :], gbuf[...])
        sq[rows, :] = mm(ones_diag, qbuf[...])

    even_bufs, odd_bufs = (ga, qa, ba, ca), (gb, qb, bb, cc)

    def back_pair(mm_, carry):
        m = pairs - 1 - mm_
        back_sums(jnp.minimum(2 * m + 2, chunks - 1), *even_bufs)
        carry = back_chunk(2 * m + 1, carry, odd, odd_at(m), even, even_at(m) + span - states, *odd_bufs)
        back_sums(2 * m + 1, *odd_bufs)
        flow, acc = back_chunk(2 * m, carry, even, even_at(m), odd, even_at(m), *even_bufs)
        return tuple(flow), tuple(acc)

    def out_block(b, carry):
        at = pl.multiple_of(b * STEP, STEP)
        rows = pl.ds(at, STEP)
        total = outp[pl.ds(mine + at, STEP), :] + outr[rows, :]
        out[rows, :] = (tok[rows, :].astype(f32) + total).astype(bf16)
        return carry

    stops = [pairs * p // 8 for p in (0, 2, 4, 6, 8)]
    carry = (zeros, zeros)
    carry = lax.fori_loop(stops[0], stops[1], back_pair, carry)
    out_copy.wait_recv()
    lax.fori_loop(0, tl // STEP, out_block, 0)
    carry = lax.fori_loop(stops[1], stops[2], back_pair, carry)
    for copy in relays:
        copy.wait_recv()
    z_out = partial_sum(0, fac_out)
    carry = lax.fori_loop(stops[2], stops[3], back_pair, carry)
    z_gate = partial_sum(1, fac_gate)
    carry = lax.fori_loop(stops[3], stops[4], back_pair, carry)
    back_sums(0, *even_bufs)
    acc = carry[1]
    g_out = total_sum(0, z_out)

    def dpre_block(b, carry):
        at = pl.ds(pl.multiple_of(b * STEP, STEP), STEP)
        sums, gains = [], []
        for n, sl in enumerate(halves):
            flow, value, dy = du[at, sl], act[at, sl], dyf[at, sl]
            dpre = (sq[at, sl] + flow * value) * sig[at, sl]
            dpl[at, sl] = dpre.astype(bf16)
            du[at, sl] = flow * s1[at, sl] + skip_own[:, sl] * dy
            both = dy * value
            sums.append(carry[0][n] + dpre[0:8] + dpre[8:16])
            gains.append(carry[1][n] + both[0:8] + both[8:16])
        return tuple(sums), tuple(gains)

    none = tuple(jnp.zeros((8, half), f32) for _ in halves)
    sums, gains = lax.fori_loop(0, chunks, dpre_block, (none, none))
    first = nproj + rank + states
    line_conv, line_cb, line_dtb, line_skip, line_gain = (
        first,
        first + taps,
        first + taps + 1,
        first + taps + 2,
        first + taps + 3,
    )
    for n, sl in enumerate(halves):
        sm[line_dtb : line_dtb + 1, sl] = jnp.sum(sums[n], axis=0, keepdims=True)
        sm[line_skip : line_skip + 1, sl] = jnp.sum(gains[n], axis=0, keepdims=True)
    for j in range(tiles):
        sl = slice(j * LANES, (j + 1) * LANES)
        sm[nproj + rank : first, sl] = acc[j] * rates[j]

    late = sum(dyf[t - 1 : t, sl] * final[j] for j, sl in enumerate(tile))
    for k in range(chunks):
        cols = slice(k * STEP, (k + 1) * STEP)
        tsc[rank : rank + states, cols] = dbt[k][:, 0:STEP]
        tsc[rank + states : nproj, cols] = dct[k][:, 0:STEP]
    shifted = pltpu.roll(tsc[rank + states : nproj, :], t - 1, 1)
    at_end = lax.broadcasted_iota(jnp.int32, (states, t), 1) == t - 1
    tsc[rank + states : nproj, :] = jnp.where(
        at_end, jnp.sum(late, axis=1, keepdims=True), shifted
    )
    pp2[...] = tsc[...].T
    pp2[:, 0:rank] = mm(dpl[...], dtw_own, NT)
    dproj_copy = send(next(ids), pp2, pq2, row, other)
    for sl in lane_tiles(w, 2 * LANES):
        sm[nproj : nproj + rank, sl] = mm(rank_turned, dpl[:, sl])
    g_gate = total_sum(1, z_gate)
    pass_on(g_out, 1)
    dproj_copy.wait_recv()
    dproj = pp2[...] + pq2[...]
    dproj_low = dproj[:, 0:nproj].astype(bf16)
    dproj_turned = dproj.T[0:nproj, :].astype(bf16)
    for sl in lane_tiles(w, 2 * LANES):
        sq[:, sl] = mm(dproj_low, xw_own[:, sl])

    def dconv_block(b, carry):
        at = pl.multiple_of(b * STEP, STEP)
        view = inner.at[pl.ds(at, STEP + 8)]
        rows = pl.ds(at, STEP)
        masks = mcol[rows, :]
        sums = [list(v) for v in carry]
        for n, sl in enumerate(halves):
            grad = (du[rows, sl] + sq[rows, sl]) * dsilu[rows, sl]
            dconv[rows, sl] = grad
            terms = [grad, grad * view[8 : 8 + STEP, sl]]
            for j in range(1, taps):
                terms.append(grad * masks[:, j - 1 : j] * view[8 - j : 8 - j + STEP, sl])
            for m, term in enumerate(terms):
                sums[m][n] = sums[m][n] + term[0:8] + term[8:16]
        return tuple(tuple(v) for v in sums)

    sums = lax.fori_loop(0, chunks, dconv_block, (none,) * (taps + 1))
    for n, sl in enumerate(halves):
        sm[line_cb : line_cb + 1, sl] = jnp.sum(sums[0][n], axis=0, keepdims=True)
        for j in range(taps):
            at = line_conv + taps - 1 - j
            sm[at : at + 1, sl] = jnp.sum(sums[1 + j][n], axis=0, keepdims=True)

    def dinner_block(b, carry):
        at = pl.multiple_of(b * STEP, STEP)
        view = dconv.at[pl.ds(at, STEP + 8)]
        masks = mcol.at[pl.ds(at, STEP + 8)]
        for sl in halves:
            total = cw_own[taps - 1 : taps, sl] * view[0:STEP, sl]
            for j in range(1, taps):
                tap = cw_own[taps - 1 - j : taps - j, sl]
                total = total + tap * view[j : j + STEP, sl] * masks[j : j + STEP, j - 1 : j]
            dil[pl.ds(at, STEP), sl] = total.astype(bf16)
        return carry

    lax.fori_loop(0, chunks, dinner_block, 0)
    fac_in = send_factors(2, dil)
    for sl in lane_tiles(d, 2 * LANES):
        dn[:, sl] = dn[:, sl] + mm(dil[...], win_i[sl, :], NT)
    dn_copy = send(next(ids), dn.at[pl.ds(theirs, tl), :], dnr, row, other)
    for sl in lane_tiles(w, 2 * LANES):
        sm[0:nproj, sl] = mm(dproj_turned, actl[:, sl])
    pass_on(g_out, 2)
    pass_on(g_out, 3)
    for s in (0, 1):
        pass_across(g_out, s)
    dn_copy.wait_recv()

    def norm_back(b, carry):
        at = pl.multiple_of(b * STEP, STEP)
        rows = pl.ds(at, STEP)
        values = tok[rows, :].astype(f32)
        scale = lax.rsqrt(jnp.mean(values * values, axis=-1, keepdims=True) + EPS)
        unit_rows = values * scale
        grad = dn[pl.ds(mine + at, STEP), :] + dnr[rows, :]
        inside = grad * gain_row
        mean = jnp.mean(inside * unit_rows, axis=-1, keepdims=True)
        both = grad * unit_rows
        gtok[rows, :] = (cot[rows, :].astype(f32) + scale * (inside - unit_rows * mean)).astype(bf16)
        return carry + both[0:8] + both[8:16]

    total = lax.fori_loop(0, tl // STEP, norm_back, jnp.zeros((8, d), f32))
    sm[line_gain : line_gain + 1, :] = jnp.sum(total, axis=0, keepdims=True)
    count = sm.shape[0]
    for j, sl in enumerate(tile):
        smb[j * count : (j + 1) * count, :] = sm[:, sl].astype(bf16)
        smf[j * count : (j + 1) * count, :] = sm[:, sl]
    smf[tiles * count :, :] = jnp.zeros((smf.shape[0] - tiles * count, LANES), f32)

    squarter = smb.shape[0] // PLANE
    szrows = squarter // DEPTH
    over_plane = [
        send(
            next(ids), smb.at[block(plane_place(s), squarter), :], sfac.at[s - 1], plane_row(s), core
        )
        for s in range(1, PLANE)
    ]
    for s in (1, 2, 3):
        pass_on(g_gate, s)
    z_in = partial_sum(2, fac_in)
    for s in (2, 3):
        pass_across(g_out, s)
    for copy in over_plane:
        copy.wait_recv()
    total = smf[block(place, squarter), :]
    for s in range(PLANE - 1):
        total = total + sfac[s].astype(f32)
    smf[block(place, squarter), :] = total
    smb_sum = sres.at[block(place, squarter), :]
    smb_sum[...] = total.astype(bf16)
    over_z = [
        send(
            next(ids),
            sres.at[pl.ds(pl.multiple_of(place * squarter + z_place(s) * szrows, szrows), szrows), :],
            szr.at[s - 1],
            z_row(s),
            core,
        )
        for s in range(1, DEPTH)
    ]
    for s in (0, 1, 2, 3):
        pass_across(g_gate, s)
    twin_out = finish(g_out)
    g_in = total_sum(2, z_in)
    for copy in over_z:
        copy.wait_recv()
    own_small = pl.ds(pl.multiple_of(place * squarter + pz * szrows, szrows), szrows)
    total = smf[own_small, :]
    for s in range(DEPTH - 1):
        total = total + szr[s].astype(f32)
    sown[...] = total.astype(bf16)
    small_along = [
        send(next(ids), sown, sfin.at[own_small, :], z_row(s), core) for s in range(1, DEPTH)
    ]
    sfin[own_small, :] = sown[...]
    twin_gate = finish(g_gate)
    for s in (1, 2, 3):
        pass_on(g_in, s)
    for copy in small_along:
        copy.wait_recv()
    part = sfin.at[block(place, squarter), :]
    small_near = [send(next(ids), part, part, plane_row(s), core) for s in range(1, PLANE)]
    for s in (0, 1, 2, 3):
        pass_across(g_in, s)
    for copy in small_near:
        copy.wait_recv()
    small_place = small.at[block(core, smb.shape[0]), :]
    small_copy = pltpu.make_async_copy(sfin, small_place, ls.at[6])
    small_copy.start()
    locals_.append(small_copy)
    twin_small = send(next(ids), sfin, small_place, row, other)
    twin_in = finish(g_in)
    for copy in (twin_out, twin_gate, twin_small, twin_in):
        copy.wait_recv()
    for copy in locals_:
        copy.wait()
    for copy in pending:
        copy.wait_send()


def wide_kernel(tiles, gin, gout, small, gin_f, gout_f, *rows):
    gin_f[...] = gin[...].T.astype(f32)
    gout_f[...] = gout[...].astype(f32)

    @pl.when(pl.program_id(0) == 0)
    def _():
        cores = rows[0].shape[1] // (tiles * LANES)
        stride = small.shape[0] // cores
        matrices = [ref for ref in rows if len(ref.shape) == 2]
        vectors = [ref for ref in rows if len(ref.shape) == 1]
        count = sum(ref.shape[0] for ref in matrices) + len(vectors)
        pad = -(-count // 32) * 32
        last = [None] * tiles
        for n in range(cores * tiles):
            first = (n // tiles) * stride + (n % tiles) * pad
            value = small[first : first + pad, :].astype(f32)
            cols = slice(n * LANES, (n + 1) * LANES)
            at = 0
            for ref in matrices:
                ref[:, cols] = value[at : at + ref.shape[0], :]
                at += ref.shape[0]
            for ref in vectors[:-1]:
                ref[cols] = value[at : at + 1, :].reshape(LANES)
                at += 1
            piece = value[at : at + 1, :]
            j = n % tiles
            last[j] = piece if last[j] is None else last[j] + piece
        for j in range(tiles):
            vectors[-1][j * LANES : (j + 1) * LANES] = last[j].reshape(LANES)


def local(
    tokens, marks, norm_gain, in_weight, conv_weight, conv_bias, x_weight, dt_weight,
    dt_bias, a_log, skip, out_weight, cotangent,
):
    tl, d = tokens.shape[1:]
    e = out_weight.shape[0]
    w = e // lax.axis_size("seq")
    t = tl * lax.axis_size("seq")
    states, rank, nproj, taps = a_log.shape[0], dt_weight.shape[0], x_weight.shape[0], conv_weight.shape[0]
    chunks, span, tiles = t // STEP, STEP * states, w // LANES
    quarter = w // PLANE
    zrows = quarter // DEPTH
    lines = -(-(nproj + rank + states + taps + 4) // 32) * 32
    slines = -(-lines * tiles // (16 * TEAM)) * 16 * TEAM
    vmem = pl.BlockSpec(memory_space=pltpu.VMEM)
    anywhere = pl.BlockSpec(memory_space=pl.ANY)
    wide = pltpu.VMEM((t, w), f32)
    low = pltpu.VMEM((t, w), bf16)
    one = pltpu.VMEM((t, LANES), f32)
    scratch = [
        pltpu.VMEM((d, w), bf16), pltpu.VMEM((d, w), bf16), pltpu.VMEM((w, d), bf16),
        pltpu.VMEM((2, t, d), bf16), pltpu.VMEM((PLANE - 1, 2, t, d), bf16),
        pltpu.VMEM((8, t), f32), pltpu.VMEM((t + 8, LANES), f32), pltpu.VMEM((8, e), f32),
        pltpu.VMEM((t + 8, w), f32), wide, wide, wide, wide, low, wide, wide, wide, wide, wide, wide, wide,
        one, one, one, one, pltpu.VMEM((LANES, t), f32),
        pltpu.VMEM((t * states // 2, w), bf16), pltpu.VMEM((t * states // 2 + states, w), bf16),
        pltpu.VMEM((chunks, states, LANES), f32), pltpu.VMEM((chunks, states, LANES), f32),
        pltpu.VMEM((t, span), bf16), pltpu.VMEM((t, span), bf16),
        *[pltpu.VMEM((span, w), bf16)] * 4, *[pltpu.VMEM((span, LANES), bf16)] * 4,
        *[pltpu.VMEM((chunks, states, LANES), f32)] * 2,
        low, low, low, low, pltpu.VMEM((3, w, t), bf16), pltpu.VMEM((t + 8, w), f32),
        pltpu.VMEM((t, d), f32), pltpu.VMEM((tl, d), f32),
        pltpu.VMEM((t, d), f32), pltpu.VMEM((tl, d), f32),
        pltpu.VMEM((3, PLANE - 1, quarter, t), bf16), pltpu.VMEM((quarter, d), f32),
        pltpu.VMEM((3, zrows, d), f32), pltpu.VMEM((3, quarter, d), bf16),
        pltpu.VMEM((3, DEPTH - 1, zrows, d), bf16), pltpu.VMEM((3, w, d), bf16),
        pltpu.VMEM((lines, w), f32), pltpu.VMEM((slines, LANES), bf16), pltpu.VMEM((slines, LANES), f32),
        pltpu.VMEM((PLANE - 1, slines // PLANE, LANES), bf16),
        pltpu.VMEM((DEPTH - 1, slines // TEAM, LANES), bf16),
        pltpu.VMEM((slines, LANES), bf16), pltpu.VMEM((slines // TEAM, LANES), bf16),
        pltpu.VMEM((slines, LANES), bf16),
        pltpu.SemaphoreType.DMA((8,)),
        pltpu.SemaphoreType.DMA((112,)), pltpu.SemaphoreType.DMA((112,)),
    ]
    cores = e // w
    output, grad_tokens, gin, gout, small = pl.pallas_call(
        body_kernel,
        out_shape=[
            jax.ShapeDtypeStruct((tl, d), bf16),
            jax.ShapeDtypeStruct((tl, d), bf16),
            jax.ShapeDtypeStruct((2 * e, d), bf16),
            jax.ShapeDtypeStruct((e, d), bf16),
            jax.ShapeDtypeStruct((cores * slines, LANES), bf16),
        ],
        in_specs=[vmem, vmem, vmem, anywhere] + [vmem] * 7 + [anywhere, vmem],
        out_specs=[vmem, vmem, anywhere, anywhere, anywhere],
        scratch_shapes=scratch,
        compiler_params=pltpu.CompilerParams(
            collective_id=0, has_side_effects=True, vmem_limit_bytes=60 * 2**20
        ),
        name="block",
    )(
        tokens.reshape(tl, d), marks.reshape(1, tl), norm_gain, in_weight, conv_weight,
        conv_bias, x_weight, dt_weight, dt_bias, a_log, skip, out_weight, cotangent.reshape(tl, d),
    )

    steps = 8
    shapes = [(nproj, e), (rank, e), (states, e), (taps, e), (e,), (e,), (e,), (d,)]
    once = [pl.BlockSpec(s, functools.partial(lambda k, i: (0,) * k, len(s))) for s in shapes]
    gout_spec = pl.BlockSpec((e // steps, d), lambda i: (i, 0))
    grads = pl.pallas_call(
        functools.partial(wide_kernel, tiles),
        grid=(steps,),
        out_shape=[jax.ShapeDtypeStruct(s, f32) for s in [(d, 2 * e), (e, d)] + shapes],
        in_specs=[
            pl.BlockSpec((2 * e // steps, d), lambda i: (i, 0)),
            gout_spec,
            pl.BlockSpec((cores * slines, LANES), lambda i: (0, 0)),
        ],
        out_specs=[pl.BlockSpec((d, 2 * e // steps), lambda i: (0, i)), gout_spec] + once,
        compiler_params=pltpu.CompilerParams(vmem_limit_bytes=60 * 2**20),
        name="widen",
    )(gin, gout, small)
    rows = lax.axis_size("rows")
    if rows > TEAM:
        grads = [v * (1.0 / TEAM) for v in lax.psum(grads, "rows")]
    grad_in, grad_out, grad_x, grad_dt, grad_log, grad_conv, g_cb, g_dtb, g_skip, g_gain = grads
    return (
        output[None], grad_tokens[None], g_gain, grad_in, grad_conv, g_cb, grad_x, grad_dt, g_dtb, grad_log,
        g_skip, grad_out,
    )


def solution(mesh):
    split = P("rows", "seq", None)
    whole = P()
    in_specs = (split, P("rows", "seq")) + (whole,) * 10 + (split,)
    out_specs = (split, split) + (whole,) * 10
    return jax.shard_map(local, mesh=mesh, in_specs=in_specs, out_specs=out_specs, check_vma=False)
```

time: 136 us -> 106 us (0.78)
  Pallas kernels: 121 us -> 104 us
  local copies, waits for them, and re-layouts: 11.5 us -> 1.36 us
  other arithmetic: 2.46 us -> 0 us
    pallas_call x1, Pallas kernels: 115 us -> 93.2 us  [local(): pl.pallas_call(body_kernel, out_shape=[jax.ShapeDtypeStruct((tl, d), bf16...]
    reshape x4 -> x0, local copies, waits for them, and re-layouts: 5.15 us -> none  [the longest x1 1.29 us: local(): dt_bias.reshape(1, e)]
    unnamed x12 -> x6, local copies, waits for them, and re-layouts: 6.39 us -> 1.36 us
    pallas_call x1, Pallas kernels: 6.09 us -> 10.5 us  [local(): pl.pallas_call(functools.partial(wide_kernel, tiles), grid=(steps,), out_...]
    pallas_call x4 -> x0, other arithmetic: 2.46 us -> none  [local(): pl.pallas_call(wide_kernel, grid=(steps,), out_shape=[jax.ShapeDtypeStruc...]
where the time goes in v1:
time: 106 us
  Pallas kernels  104 us (98%)
  local copies, waits for them, and re-layouts  1.36 us (1%)
    pallas_call x1, Pallas kernels, local(): pl.pallas_call(body_kernel, out_shape=[jax.ShapeDtypeStruct((tl, d), bf16...  93.2 us
    pallas_call x1, Pallas kernels, local(): pl.pallas_call(functools.partial(wide_kernel, tiles), grid=(steps,), out_...  10.5 us

profile of v1, /device:TPU:1, one launch (start us, length us, event | category | flops | bytes accessed | tf_op | source)
XLA Modules:
  0.0 105.7 jit_solution(16745585843394107410)
XLA Ops:
  0.6 93.2 %block.1 = (bf16[128,768]{1,0:T(8,128)(2,1)}, bf16[128,768]{1,0:T(8,128)(2,1)}, bf16[3072,768]{1,0:T(8,128)(2,1)}, bf16[1536,768]{1,0:T(8,128)(2,1)}, bf16[2048,128]{1,0:T(8,128)(2,1)}) custom-call(bf16[128,768]{1,0:T(8,128)(2,1)} %bitcast.6, s32[1,128]{1,0:T(1,128)} %marks.1, f32[768]{0:T(1024)} %gain.1, bf16[768,3072]{1,0:T(8,128)(2,1)} %win.1, ...), custom_call_target="tpu_custom_call" | custom-call | tf_op jit(solution)/shard_map/block/pallas_call | solution.py:758
  93.8 0.0 copy-start.1
  93.8 0.0 copy-start
  93.8 10.5 %widen.1 = (f32[768,3072]{1,0:T(8,128)}, f32[1536,768]{1,0:T(8,128)}, f32[80,1536]{1,0:T(8,128)}, f32[48,1536]{1,0:T(8,128)}, f32[16,1536]{1,0:T(8,128)}, /*inde...) custom-call(bf16[3072,768]{1,0:T(8,128)(2,1)} %get-tuple-element.29.gin, ...), custom_call_target="tpu_custom_call" | custom-call | tf_op jit(solution)/shard_map/widen/pallas_call | solution.py:783
  104.3 0.0 copy-done.1
  104.3 0.7 copy.27
  105.0 0.0 copy-done
  105.0 0.7 copy.28
Async XLA Ops:
  93.8 10.5 %copy-start.1 = (bf16[128,768]{1,0:T(8,128)(2,1)S(1)}, bf16[128,768]{1,0:T(8,128)(2,1)}, u32[]{:S(2)}) copy-start(bf16[128,768]{1,0:T(8,128)(2,1)} %get-tuple-element.27) | copy-start | bytes 589828
  93.8 11.2 %copy-start = (bf16[128,768]{1,0:T(8,128)(2,1)S(1)}, bf16[128,768]{1,0:T(8,128)(2,1)}, u32[]{:S(2)}) copy-start(bf16[128,768]{1,0:T(8,128)(2,1)} %get-tuple-element.28) | copy-start | bytes 589828

commit v2 on v1

v2 whole, which is shorter than its diff:
```python
import functools

import jax
import jax.numpy as jnp
from jax import lax
from jax.experimental import pallas as pl
from jax.experimental.pallas import tpu as pltpu
from jax.sharding import PartitionSpec as P

f32 = jnp.float32
bf16 = jnp.bfloat16
EPS = 1e-05
LANES = 128
STEP = 16
PLANE = 4
DEPTH = 4
TEAM = PLANE * DEPTH
MESH = pl.DeviceIdType.MESH
NN = (((1,), (0,)), ((), ()))
NT = (((1,), (1,)), ((), ()))


def mm(a, b, dims=NN):
    return lax.dot_general(a, b, dims, preferred_element_type=f32)


def lane_tiles(width, size):
    return [slice(j, j + size) for j in range(0, width, size)]


def body_kernel(
    tok, marks, gain_in, win, cw_in, cb_in, xw_in, dtw_in, dtb_in, alog_in, skip_in, wout, cot,
    out, gtok, gout, ggate, gmix,
    win_i, win_g, wo, gain, cw, cb, xw, dtw, dtb, alog, skip, mkraw, ng, ngh, mk, mcol, lines,
    inner, gate, dgated, act, dsilu, actl, ddec, u, sig, dyf, du, s1, sq,
    pp, pq, pp2, pq2, tsc, even, odd, bt, ct, cbd, bbd, ga, gb, qa, qb, ba, bb, ca, cc, dbt, dct, lastc, tot,
    gt, dgl, dpl, dil, turn, dconv, dn, dnr, outp, outr,
    fac, pw, pown, pb, zr, sm, smb, sms, sfac, spb, szr,
    ls, ss, rs,
):
    row, core = lax.axis_index("rows"), lax.axis_index("seq")
    other = 1 - core
    team = row - row % TEAM
    px, py, pz = row % 2, (row // 2) % 2, (row // PLANE) % DEPTH
    tl, d = out.shape
    t = 2 * tl
    w = wo.shape[0]
    states = alog.shape[0]
    rank = dtw.shape[0]
    nproj = xw.shape[0]
    half = w // 2
    quarter = w // PLANE
    zrows = quarter // DEPTH
    extra, packed = smb.shape[0] // TEAM, smb.shape[1]
    place = row % PLANE
    chunks = t // STEP
    tiles = w // LANES
    mine = pl.multiple_of(core * tl, tl)
    theirs = pl.multiple_of(other * tl, tl)
    chan = pl.multiple_of(core * w, w)
    halves = lane_tiles(w, half)
    pending = []

    def flip(low, high, s):
        a, b = s % 2, s // 2
        return (high + b - 2 * b * high) * 2 + low + a - 2 * a * low

    plane_place = [flip(px, py, s) for s in range(PLANE)]
    plane_row = [team + pz * PLANE + plane_place[s] for s in range(PLANE)]
    z_place = [flip(pz % 2, pz // 2, s) for s in range(DEPTH)]
    z_row = [team + z_place[s] * PLANE + place for s in range(DEPTH)]
    ids = iter(range(10_000))

    class Send:
        def __init__(self, refs, to_row, to_core):
            self.refs, self.to, self.k = refs, (to_row, to_core), next(ids)
            self.copy().start()
            pending.append(self)

        def copy(self):
            src, dst = self.refs()
            return pltpu.make_async_remote_copy(
                src_ref=src,
                dst_ref=dst,
                send_sem=ss.at[self.k],
                recv_sem=rs.at[self.k],
                device_id=self.to,
                device_id_type=MESH,
            )

        def wait_recv(self):
            self.copy().wait_recv()

        def wait_send(self):
            self.copy().wait_send()

    def block(index, size):
        return pl.ds(pl.multiple_of(index * size, size), size)

    own = pl.ds(chan, w)
    sources = [
        (tok, ng.at[2, pl.ds(mine, tl), :]),
        (marks, mkraw.at[0:1]),
        (gain_in, gain),
        (win.at[:, own], win_i),
        (cw_in.at[:, own], cw),
        (cb_in, cb),
        (cot, ng.at[1, pl.ds(mine, tl), :]),
        (xw_in.at[:, own], xw),
        (win.at[:, pl.ds(pl.multiple_of(2 * w + core * w, w), w)], win_g),
        (wout.at[own, :], wo),
        (dtw_in.at[:, own], dtw),
        (dtb_in, dtb),
        (skip_in, skip),
        (alog_in.at[:, own], alog),
    ]
    loads = [pltpu.make_async_copy(src, dst, ls.at[n]) for n, (src, dst) in enumerate(sources)]
    for copy in loads:
        copy.start()

    barrier = pltpu.get_barrier_semaphore()
    partners = [(row, other)]
    partners += [(plane_row[s], core) for s in range(1, PLANE)]
    partners += [(z_row[s], core) for s in range(1, DEPTH)]
    for partner in partners:
        pl.semaphore_signal(barrier, inc=1, device_id=partner, device_id_type=MESH)
    pl.semaphore_wait(barrier, len(partners))

    def pair_to(ref):
        return lambda: (ref(), ref())

    def own_rows(kind):
        return ng.at[kind, pl.ds(mine, tl), :]

    def slot(s, kind, first=0, count=tl):
        return ngh.at[s - 1, kind, pl.ds(pl.multiple_of(mine + first, count), count), :]

    twin = [
        Send(lambda n=n, ref=ref: (ref, ng.at[n, pl.ds(mine, tl), :]), row, other)
        for n, ref in ((2, tok), (1, cot))
    ]
    twin.append(Send(lambda: (marks, mkraw.at[1:2]), row, other))
    early, across, relays = {}, {}, {0: [], 1: []}
    piece = tl // 2

    def share(kind):
        early[kind] = [
            Send(lambda s=s: (cot if kind else own_rows(kind), slot(s, kind)), plane_row[s], core)
            for s in (1, 2)
        ]

    def share_on(kind):
        across[kind] = []
        for s in (1, 2):
            early[kind][s - 1].wait_recv()
            first = (s - 1) * piece
            refs = lambda s=s, first=first: (slot(s, kind, first, piece), slot(3, kind, first, piece))
            across[kind].append(Send(refs, plane_row[3 - s], core))
            relays[kind].append(Send(pair_to(lambda s=s: slot(s, kind)), row, other))

    def share_end(kind):
        for s in (1, 2):
            across[kind][s - 1].wait_recv()
            refs = pair_to(lambda first=(s - 1) * piece: slot(3, kind, first, piece))
            relays[kind].append(Send(refs, row, other))

    share(1)

    for copy in loads[:3]:
        copy.wait()
    count = gain.shape[0]
    lines[0:1, 0:count] = gain[...].reshape(1, count)
    unit = 2 * STEP

    def norm_rows(first):
        gain_row = lines[0:1, 0:d]

        def norm_block(b, carry):
            at = pl.ds(pl.multiple_of(first + b * unit, unit), unit)
            rows = ng[2, at, :].astype(f32)
            scale = lax.rsqrt(jnp.mean(rows * rows, axis=-1, keepdims=True) + EPS)
            ng[0, at, :] = (rows * scale * gain_row).astype(bf16)
            return carry

        lax.fori_loop(0, tl // unit, norm_block, 0)

    norm_rows(mine)
    share(0)

    inner[0:8, :] = jnp.zeros((8, w), f32)
    dconv[t : t + 8, :] = jnp.zeros((8, w), f32)
    mcol[t : t + 8, :] = jnp.zeros((8, LANES), f32)
    odd[0:states, :] = jnp.zeros((states, w), bf16)
    tsc[...] = jnp.zeros(tsc.shape, f32)
    tot[...] = jnp.zeros(tot.shape, f32)
    smb[...] = jnp.zeros(smb.shape, bf16)
    sms[...] = jnp.zeros(sms.shape, f32)
    for ref in (ga, qa, ba, ca):
        ref[...] = jnp.zeros(ref.shape, bf16)
    sm[...] = jnp.zeros(sm.shape, f32)

    for copy in twin:
        copy.wait_recv()
    norm_rows(theirs)
    own_marks, twin_marks = mkraw[0:1, :].astype(f32), mkraw[1:2, :].astype(f32)
    mk[:, pl.ds(mine, tl)] = jnp.broadcast_to(own_marks, (8, tl))
    mk[:, pl.ds(theirs, tl)] = jnp.broadcast_to(twin_marks, (8, tl))
    for copy in loads[3:7]:
        copy.wait()

    for sl in lane_tiles(w, 2 * LANES):
        inner[8 : 8 + t, sl] = mm(ng[0], win_i[:, sl]).astype(bf16).astype(f32)

    lane = lax.broadcasted_iota(jnp.int32, (8, t), 1)
    mark = mk[...]
    keep = jnp.where(lane == 0, 0.0, 1.0 - mark)
    mask2 = keep * pltpu.roll(keep, 1, 1)
    mask3 = mask2 * pltpu.roll(keep, 2, 1)
    line = lax.broadcasted_iota(jnp.int32, (LANES, t), 0)

    def spread(v):
        return jnp.broadcast_to(v[0:1, :], (LANES, t))

    stacked = jnp.where(line == 0, spread(keep), 0.0)
    stacked = jnp.where(line == 1, spread(mask2), stacked)
    stacked = jnp.where(line == 2, spread(mask3), stacked)
    stacked = jnp.where(line == 3, spread(mark), stacked)
    mcol[0:t, :] = stacked.T

    for copy in loads[7:]:
        copy.wait()
    for n, ref in enumerate((gain, cb, dtb, skip)):
        count = ref.shape[0]
        lines[n : n + 1, 0:count] = ref[...].reshape(1, count)
    cw_own = cw[...]
    cb_own = lines[1:2, pl.ds(chan, w)]
    taps = cw.shape[0]

    def conv_block(b, carry):
        at = pl.multiple_of(b * STEP, STEP)
        view = inner.at[pl.ds(at, STEP + 8)]
        masks = mcol[pl.ds(at, STEP), :]
        for sl in halves:
            total = cb_own[:, sl] + cw_own[taps - 1 : taps, sl] * view[8 : 8 + STEP, sl]
            for j in range(1, taps):
                tap = cw_own[taps - 1 - j : taps - j, sl]
                total = total + tap * view[8 - j : 8 - j + STEP, sl] * masks[:, j - 1 : j]
            sg = 1.0 / (1.0 + jnp.exp(-total))
            value = total * sg
            act[pl.ds(at, STEP), sl] = value
            actl[pl.ds(at, STEP), sl] = value.astype(bf16)
            dsilu[pl.ds(at, STEP), sl] = sg * (1.0 + total * (1.0 - sg))
        return carry

    lax.fori_loop(0, chunks, conv_block, 0)
    xw_own = xw[...]
    pp[:, 0:nproj] = mm(actl[...], xw_own, NT)
    proj_copy = Send(lambda: (pp, pq), row, other)

    for sl in lane_tiles(w, 2 * LANES):
        gate[:, sl] = mm(ng[0], win_g[:, sl])
        dgated[:, sl] = mm(ng[1], wo[sl, :], NT)

    def dy_block(b, carry):
        at = pl.ds(pl.multiple_of(b * STEP, STEP), STEP)
        for sl in halves:
            g = gate[at, sl]
            low = (dgated[at, sl] * (g / (1.0 + jnp.exp(-g)))).astype(bf16)
            dyf[at, sl] = low.astype(f32)
        return carry

    lax.fori_loop(0, chunks, dy_block, 0)

    share_on(1)

    proj_copy.wait_recv()
    proj = pp[...] + pq[...]
    turned = proj.T
    for k in range(chunks):
        cols = slice(k * STEP, (k + 1) * STEP)
        bt[k, :, 0:STEP] = turned[rank : rank + states, cols]
        ct[k, :, 0:STEP] = turned[rank + states : rank + 2 * states, cols]
    rank_low = proj[:, 0:rank].astype(bf16)
    rank_turned = turned[0:rank, :].astype(bf16)
    dtw_own = dtw[...]
    dtb_own = lines[2:3, pl.ds(chan, w)]
    for sl in lane_tiles(w, 2 * LANES):
        sig[:, sl] = mm(rank_low, dtw_own[:, sl]) + dtb_own[:, sl]

    def delta_block(b, carry):
        at = pl.ds(pl.multiple_of(b * STEP, STEP), STEP)
        marked = mcol[at, :][:, 3:4] > 0.5
        for sl in halves:
            pre = sig[at, sl]
            e = jnp.exp(-jnp.abs(pre))
            one = 1.0 + e
            log1p = jnp.where(one == 1.0, e, jnp.log(one) * (e / (one - 1.0)))
            delta = jnp.maximum(pre, 0.0) + log1p
            sig[at, sl] = jnp.where(pre >= 0.0, 1.0, e) / one
            inflow = delta * act[at, sl]
            u[at, sl] = inflow
            s1[at, sl] = delta
            ddec[at, sl] = jnp.where(marked, 1e30, delta)
        return carry

    lax.fori_loop(0, chunks, delta_block, 0)

    span = STEP * states
    pick = (
        lax.broadcasted_iota(jnp.int32, (states, span), 0)
        == lax.broadcasted_iota(jnp.int32, (states, span), 1) % states
    ).astype(bf16)
    diag = (
        lax.broadcasted_iota(jnp.int32, (t, span), 0) % STEP
        == lax.broadcasted_iota(jnp.int32, (t, span), 1) // states
    )
    ones_diag = diag[0:STEP].astype(bf16)
    b_low = proj[:, rank : rank + states].astype(bf16)
    c_low = proj[:, rank + states : rank + 2 * states].astype(bf16)
    bbd[...] = jnp.where(diag, mm(b_low, pick), 0.0).astype(bf16)
    cbd[...] = jnp.where(diag, mm(c_low, pick), 0.0).astype(bf16)

    rates = [-jnp.exp(alog[:, j * LANES : (j + 1) * LANES]) for j in range(tiles)]
    zeros = tuple(jnp.zeros((states, LANES), f32) for _ in range(tiles))
    tile = [slice(j * LANES, (j + 1) * LANES) for j in range(tiles)]

    def even_at(m):
        return pl.multiple_of(m * span, span)

    def odd_at(m):
        return pl.multiple_of(states + m * span, states)

    def state_block(ref, first, i):
        return ref.at[pl.ds(pl.multiple_of(first + i * states, states), states)]

    def scan_chunk(k, state, kept, first):
        rows = pl.ds(pl.multiple_of(k * STEP, STEP), STEP)
        b_here, dec, flow = bt[k], ddec.at[rows], u.at[rows]
        state = list(state)
        for i in range(STEP):
            b_wide = jnp.broadcast_to(b_here[:, i : i + 1], (states, LANES))
            dest = state_block(kept, first, i)
            for j, sl in enumerate(tile):
                decay = jnp.exp(dec[i : i + 1, sl] * rates[j])
                state[j] = decay * state[j] + flow[i : i + 1, sl] * b_wide
                dest[:, sl] = state[j].astype(bf16)
        return state

    def read_chunk(k, kept, first):
        rows = pl.ds(pl.multiple_of(k * STEP, STEP), STEP)
        du[rows, :] = mm(cbd[rows, :], kept[pl.ds(pl.multiple_of(first, states), span), :])


    def gated_block(b, carry):
        skip_own = lines[3:4, pl.ds(chan, w)]
        at = pl.ds(pl.multiple_of(b * STEP, STEP), STEP)
        for sl in halves:
            y = (du[at, sl] + skip_own[:, sl] * act[at, sl]).astype(bf16).astype(f32)
            g = gate[at, sl]
            sg = 1.0 / (1.0 + jnp.exp(-g))
            gt[at, sl] = (y * (g * sg)).astype(bf16)
            dgl[at, sl] = (dgated[at, sl] * y * (sg * (1.0 + g * (1.0 - sg)))).astype(bf16)
        return carry

    class Sum:
        def __init__(self, n, source):
            self.n, self.source, self.factors = n, source, []
            self.lines = zrows + (extra if n == 2 else 0)
            self.near, self.far, self.twin = [], [], []

        def send_factors(self, part):
            n, at = self.n, slice(part * tl, (part + 1) * tl)
            for sl in tile:
                turn[n, sl, at] = self.source[at, sl].T
            for s in range(1, PLANE):
                refs = lambda s=s: (
                    turn.at[n, block(plane_place[s], quarter), at],
                    fac.at[n, s - 1, :, at],
                )
                self.factors.append(Send(refs, plane_row[s], core))

        def rows(self, where, first, count):
            ref = (gout, ggate, gmix)[self.n]
            first = (core * PLANE + where) * DEPTH * self.lines + first
            return ref.at[pl.ds(pl.multiple_of(first, count), count), :]

        def shard(self, where, z):
            return self.rows(where, z * self.lines, self.lines)

        def partial(self):
            n = self.n
            for copy in self.factors:
                copy.wait_recv()
            kind = 1 if n == 0 else 0
            lefts = [turn[n, block(place, quarter), :]] + [fac[n, s] for s in range(PLANE - 1)]
            for sl in lane_tiles(d, 2 * LANES):
                total = mm(lefts[0], ng[kind, :, sl])
                for s in range(PLANE - 1):
                    total = total + mm(lefts[s + 1], ngh[s, kind, :, sl])
                pw[:, sl] = total
                pb[n, :, sl] = total.astype(bf16)
            pown[n] = pw[block(pz, zrows), :]
            self.depth = [
                Send(
                    lambda s=s: (pb.at[n, block(z_place[s], zrows), :], zr.at[n, s - 1]),
                    z_row[s],
                    core,
                )
                for s in range(1, DEPTH)
            ]

        def near_shard(self, z):
            part = pair_to(lambda: self.shard(place, z))
            self.near.append([Send(part, plane_row[s], core) for s in (1, 2)])

        def total(self):
            for copy in self.depth:
                copy.wait_recv()
            total = pown[self.n]
            for s in range(DEPTH - 1):
                total = total + zr[self.n, s].astype(f32)
            part = self.shard(place, pz)
            part[0:zrows, :] = total.astype(bf16)
            if self.n == 2:
                for copy in small_depth:
                    copy.wait_recv()
                total = sms[block(place * DEPTH + pz, extra), :]
                for s in range(DEPTH - 1):
                    total = total + szr[s].astype(f32)
                part[zrows:, 0:packed] = total.astype(bf16)
                part[zrows:, packed:] = jnp.zeros((extra, d - packed), bf16)
            own = pair_to(lambda: self.shard(place, pz))
            self.along = [Send(own, z_row[s], core) for s in (1, 2)]
            self.beyond = []
            self.near_shard(pz)

        def pass_on(self, s):
            if s < 3:
                self.along[s - 1].wait_recv()
                part = pair_to(lambda: self.shard(place, z_place[s]).at[:, halves[s - 1]])
                self.beyond.append(Send(part, z_row[3 - s], core))
            else:
                for copy in self.beyond:
                    copy.wait_recv()
            self.near_shard(z_place[s])
            if s == DEPTH - 1:
                self.to_twin(place)

        def pass_across(self, s):
            for copy in self.near[s]:
                copy.wait_recv()
            q = 1 + s % 2
            part = pair_to(lambda: self.shard(plane_place[q], z_place[s]))
            self.far.append(Send(part, plane_row[3 - q], core))
            if s == DEPTH - 1:
                for q in (1, 2):
                    self.to_twin(plane_place[q])

        def to_twin(self, where):
            self.twin.append(Send(pair_to(lambda: self.rows(where, 0, DEPTH * self.lines)), row, other))

        def finish(self):
            for copy in self.far:
                copy.wait_recv()
            self.to_twin(plane_place[3])

    sum_out, sum_gate, sum_in = Sum(0, gt), Sum(1, dgl), Sum(2, dil)

    def gated_half(part):
        lax.fori_loop(part * chunks // 2, (part + 1) * chunks // 2, gated_block, 0)
        sum_out.send_factors(part)

    pairs = chunks // 2
    odd[pl.ds(states, span), :] = jnp.zeros((span, w), bf16)

    def scan_pair(m, state):
        read_chunk(jnp.maximum(2 * m - 1, 0), odd, odd_at(jnp.maximum(m - 1, 0)))
        state = scan_chunk(2 * m, state, even, even_at(m))
        read_chunk(2 * m, even, even_at(m))
        state = scan_chunk(2 * m + 1, state, odd, odd_at(m))

        @pl.when(m == pairs // 2 - 1)
        def _():
            read_chunk(chunks // 2 - 1, odd, odd_at(pairs // 2 - 1))
            gated_half(0)
            share_on(0)

        return tuple(state)

    final = lax.fori_loop(0, pairs, scan_pair, zeros)
    read_chunk(chunks - 1, odd, odd_at(pairs - 1))
    gated_half(1)
    share_end(1)
    sum_gate.send_factors(0)
    sum_gate.send_factors(1)

    late = sum(dyf[t - 1 : t, sl] * final[j] for j, sl in enumerate(tile))
    lastc[...] = jnp.broadcast_to(jnp.sum(late, axis=1, keepdims=True), (states, LANES))

    def back_chunk(k, carry, kept, first, before, last, gbuf, qbuf, bbuf, cbuf):
        base = pl.multiple_of(k * STEP, STEP)
        rows = pl.ds(base, STEP)
        c_here, dec, dys, inflow = ct[k], ddec.at[rows], dyf.at[rows], u.at[rows]
        dys_before = dyf.at[pl.ds(pl.multiple_of(jnp.maximum(base - STEP, 0), STEP), STEP)]
        flow, acc = list(carry[0]), list(carry[1])
        for i in reversed(range(STEP)):
            c_wide = jnp.broadcast_to(c_here[:, i : i + 1], (states, LANES))
            at = slice(i * states, (i + 1) * states)
            old = state_block(kept, first, i - 1) if i else state_block(before, last, 0)
            dy_old = dys_before[STEP - 1 : STEP, :] if i == 0 else dys[i - 1 : i, :]
            for_b = for_c = None
            for j, sl in enumerate(tile):
                rate = dec[i : i + 1, sl]
                g = c_wide * dys[i : i + 1, sl] + flow[j]
                gbuf[at, sl] = g.astype(bf16)
                flow[j] = g * jnp.exp(rate * rates[j])
                h_old = old[:, sl].astype(f32)
                q = flow[j] * h_old
                acc[j] = acc[j] + q * rate
                qbuf[at, sl] = (q * rates[j]).astype(bf16)
                term_b, term_c = g * inflow[i : i + 1, sl], h_old * dy_old[:, sl]
                for_b = term_b if for_b is None else for_b + term_b
                for_c = term_c if for_c is None else for_c + term_c
            bbuf[at, :] = for_b.astype(bf16)
            cbuf[at, :] = for_c.astype(bf16)
        return flow, acc

    lane_of = lax.broadcasted_iota(jnp.int32, (states, LANES), 1)
    ones = jnp.ones((LANES, LANES), bf16)

    def back_sums(k, gbuf, qbuf, bbuf, cbuf):
        rows = pl.ds(pl.multiple_of(k * STEP, STEP), STEP)
        for parts, dest in ((bbuf, dbt), (cbuf, dct)):
            summed = mm(parts[...], ones)
            value = jnp.zeros((states, LANES), f32)
            for i in range(STEP):
                value = jnp.where(lane_of == i, summed[i * states : (i + 1) * states, :], value)
            dest[k] = value
        du[rows, :] = mm(bbd[rows, :], gbuf[...])
        sq[rows, :] = mm(ones_diag, qbuf[...])

    even_bufs, odd_bufs = (ga, qa, ba, ca), (gb, qb, bb, cc)

    def out_block(b, carry):
        at = pl.multiple_of(b * STEP, STEP)
        rows = pl.ds(at, STEP)
        total = outp[pl.ds(mine + at, STEP), :] + outr[rows, :]
        out[rows, :] = (ng[2, pl.ds(mine + at, STEP), :].astype(f32) + total).astype(bf16)
        return carry

    first = nproj + rank + states
    line_conv, line_cb, line_dtb, line_skip, line_gain = (
        first,
        first + taps,
        first + taps + 1,
        first + taps + 2,
        first + taps + 3,
    )
    tot_dtb, tot_skip, tot_conv = 0, 1, 2
    dproj_copies = {}

    def read_tot(n):
        return tuple(tot[n, :, sl] for sl in halves)

    def write_tot(n, values):
        for value, sl in zip(values, halves):
            tot[n, :, sl] = value

    def dpre_block(b, carry):
        at = pl.ds(pl.multiple_of(b * STEP, STEP), STEP)
        skip_own = lines[3:4, pl.ds(chan, w)]
        sums, gains = [], []
        for n, sl in enumerate(halves):
            flow, value, dy = du[at, sl], act[at, sl], dyf[at, sl]
            dpre = (sq[at, sl] + flow * value) * sig[at, sl]
            dpl[at, sl] = dpre.astype(bf16)
            s1[at, sl] = flow * s1[at, sl] + skip_own[:, sl] * dy
            both = dy * value
            sums.append(carry[0][n] + dpre[0:8] + dpre[8:16])
            gains.append(carry[1][n] + both[0:8] + both[8:16])
        return tuple(sums), tuple(gains)

    def projection_grads(part):
        at = slice(part * tl, (part + 1) * tl)
        span_of = (part * chunks // 2, (part + 1) * chunks // 2)
        sums, gains = lax.fori_loop(*span_of, dpre_block, (read_tot(tot_dtb), read_tot(tot_skip)))
        write_tot(tot_dtb, sums)
        write_tot(tot_skip, gains)
        for k in range(*span_of):
            cols = slice(k * STEP, (k + 1) * STEP)
            tsc[rank : rank + states, cols] = dbt[k][:, 0:STEP]
            tsc[rank + states : nproj, cols] = dct[k][:, 0:STEP]
        end = lastc[:, 0:1] if part else dct[chunks // 2][:, 0:1]
        shifted = pltpu.roll(tsc[rank + states : nproj, at], tl - 1, 1)
        at_end = lax.broadcasted_iota(jnp.int32, (states, tl), 1) == tl - 1
        tsc[rank + states : nproj, at] = jnp.where(at_end, end, shifted)
        pp2[at, :] = tsc[:, at].T
        pp2[at, 0:rank] = mm(dpl[at, :], dtw[...], NT)
        dproj_copies[part] = Send(lambda: (pp2.at[at, :], pq2.at[at, :]), row, other)

    def dconv_block(b, carry):
        at = pl.multiple_of(b * STEP, STEP)
        view = inner.at[pl.ds(at, STEP + 8)]
        rows = pl.ds(at, STEP)
        masks = mcol[rows, :]
        sums = [list(v) for v in carry]
        for n, sl in enumerate(halves):
            grad = (s1[rows, sl] + sq[rows, sl]) * dsilu[rows, sl]
            dconv[rows, sl] = grad
            terms = [grad, grad * view[8 : 8 + STEP, sl]]
            for j in range(1, taps):
                terms.append(grad * masks[:, j - 1 : j] * view[8 - j : 8 - j + STEP, sl])
            for m, term in enumerate(terms):
                sums[m][n] = sums[m][n] + term[0:8] + term[8:16]
        return tuple(tuple(v) for v in sums)

    def dinner_block(b, carry):
        at = pl.multiple_of(b * STEP, STEP)
        view = dconv.at[pl.ds(at, STEP + 8)]
        masks = mcol.at[pl.ds(at, STEP + 8)]
        cw_own = cw[...]
        for sl in halves:
            total = cw_own[taps - 1 : taps, sl] * view[0:STEP, sl]
            for j in range(1, taps):
                tap = cw_own[taps - 1 - j : taps - j, sl]
                total = total + tap * view[j : j + STEP, sl] * masks[j : j + STEP, j - 1 : j]
            dil[pl.ds(at, STEP), sl] = total.astype(bf16)
        return carry

    def inner_grads(part):
        at = slice(part * tl, (part + 1) * tl)
        span_of = (part * chunks // 2, (part + 1) * chunks // 2)
        dproj_copies[part].wait_recv()
        dproj = pp2[at, :] + pq2[at, :]
        pq2[at, :] = dproj
        dproj_low = dproj[:, 0:nproj].astype(bf16)
        for sl in lane_tiles(w, 2 * LANES):
            sq[at, sl] = mm(dproj_low, xw[:, sl])
        names = range(tot_conv, tot_conv + taps + 1)
        sums = lax.fori_loop(*span_of, dconv_block, tuple(read_tot(n) for n in names))
        for n, values in zip(names, sums):
            write_tot(n, values)
        lax.fori_loop(*span_of, dinner_block, 0)
        sum_in.send_factors(part)

    def late_half():
        back_sums(chunks // 2, *even_bufs)
        projection_grads(1)

    def out_sums():
        for copy in relays[1]:
            copy.wait_recv()
        sum_out.partial()

    def gate_sums():
        for copy in relays[0]:
            copy.wait_recv()
        sum_gate.partial()

    events = (
        (1, lambda: share_end(0)),
        (2, out_sums),
        (3, late_half),
        (5, gate_sums),
        (6, lambda: inner_grads(1)),
        (7, lambda: sum_out.total()),
    )

    def back_pair(step, carry):
        m = pairs - 1 - step
        back_sums(jnp.minimum(2 * m + 2, chunks - 1), *even_bufs)
        carry = back_chunk(2 * m + 1, carry, odd, odd_at(m), even, even_at(m) + span - states, *odd_bufs)
        back_sums(2 * m + 1, *odd_bufs)
        flow, acc = back_chunk(2 * m, carry, even, even_at(m), odd, even_at(m), *even_bufs)
        for when, event in events:
            pl.when(step == when * pairs // 8)(event)
        return tuple(flow), tuple(acc)

    carry = lax.fori_loop(0, pairs, back_pair, (zeros, zeros))
    back_sums(0, *even_bufs)
    for j, sl in enumerate(tile):
        sm[nproj + rank : first, sl] = carry[1][j] * rates[j]
    projection_grads(0)
    for sl in lane_tiles(d, 2 * LANES):
        dn[:, sl] = mm(dgl[...], win_g[sl, :], NT)
    inner_grads(0)
    sum_gate.total()
    sum_out.pass_on(1)
    sum_out.pass_on(2)
    for sl in lane_tiles(d, 2 * LANES):
        dn[:, sl] = dn[:, sl] + mm(dil[...], win_i[sl, :], NT)
    dn_copy = Send(lambda: (dn.at[pl.ds(theirs, tl), :], dnr), row, other)
    dproj_turned = pq2[...].T[0:nproj, :].astype(bf16)
    for sl in lane_tiles(w, 2 * LANES):
        sm[0:nproj, sl] = mm(dproj_turned, actl[:, sl])
        sm[nproj : nproj + rank, sl] = mm(rank_turned, dpl[:, sl])

    def put_line(line, n):
        for value, sl in zip(read_tot(n), halves):
            sm[line : line + 1, sl] = jnp.sum(value, axis=0, keepdims=True)

    put_line(line_dtb, tot_dtb)
    put_line(line_skip, tot_skip)
    put_line(line_cb, tot_conv)
    for j in range(taps):
        put_line(line_conv + taps - 1 - j, tot_conv + 1 + j)
    def gain_block(b, carry):
        rows = pl.ds(pl.multiple_of(b * STEP, STEP), STEP)
        values = ng[2, rows, :].astype(f32)
        scale = lax.rsqrt(jnp.mean(values * values, axis=-1, keepdims=True) + EPS)
        both = dn[rows, :] * (values * scale)
        return carry + both[0:8] + both[8:16]

    total = lax.fori_loop(0, chunks, gain_block, jnp.zeros((8, d), f32))
    sm[line_gain : line_gain + 1, :] = jnp.sum(total, axis=0, keepdims=True)
    across_tiles = packed // LANES
    for n in range(sm.shape[0] // 16 * tiles):
        to = slice(n // across_tiles * 16, n // across_tiles * 16 + 16)
        to_lanes = tile[n % across_tiles]
        value = sm[n // tiles * 16 : n // tiles * 16 + 16, tile[n % tiles]]
        smb[to, to_lanes] = value.astype(bf16)
        sms[to, to_lanes] = value
    srows = DEPTH * extra
    over_plane = [
        Send(
            lambda s=s: (smb.at[block(plane_place[s], srows), :], sfac.at[s - 1]),
            plane_row[s],
            core,
        )
        for s in range(1, PLANE)
    ]
    sum_in.partial()
    sum_out.pass_on(3)
    sum_gate.pass_on(1)
    sum_gate.pass_on(2)
    sum_out.pass_across(0)
    for copy in over_plane:
        copy.wait_recv()
    total = sms[block(place, srows), :]
    for s in range(PLANE - 1):
        total = total + sfac[s].astype(f32)
    sms[block(place, srows), :] = total
    spb[...] = total.astype(bf16)
    small_depth = [
        Send(lambda s=s: (spb.at[block(z_place[s], extra), :], szr.at[s - 1]), z_row[s], core)
        for s in range(1, DEPTH)
    ]
    sum_out.pass_across(1)
    sum_out.pass_across(2)
    sum_out.pass_across(3)
    sum_gate.pass_on(3)

    for sl in lane_tiles(d, 2 * LANES):
        outp[:, sl] = mm(gt[...], wo[:, sl])
    out_copy = Send(lambda: (outp.at[pl.ds(theirs, tl), :], outr), row, other)

    def norm_back(b, carry):
        at = pl.multiple_of(b * STEP, STEP)
        rows = pl.ds(at, STEP)
        values = ng[2, pl.ds(mine + at, STEP), :].astype(f32)
        scale = lax.rsqrt(jnp.mean(values * values, axis=-1, keepdims=True) + EPS)
        unit_rows = values * scale
        inside = (dn[pl.ds(mine + at, STEP), :] + dnr[rows, :]) * lines[0:1, 0:d]
        mean = jnp.mean(inside * unit_rows, axis=-1, keepdims=True)
        given = ng[1, pl.ds(mine + at, STEP), :].astype(f32)
        gtok[rows, :] = (given + scale * (inside - unit_rows * mean)).astype(bf16)
        return carry

    dn_copy.wait_recv()
    lax.fori_loop(0, tl // STEP, norm_back, 0)
    out_copy.wait_recv()
    lax.fori_loop(0, tl // STEP, out_block, 0)

    sum_in.total()
    sum_gate.pass_across(0)
    sum_gate.pass_across(1)
    sum_out.finish()
    sum_in.pass_on(1)
    sum_in.pass_on(2)
    sum_gate.pass_across(2)
    sum_gate.pass_across(3)
    sum_in.pass_on(3)
    sum_in.pass_across(0)
    sum_gate.finish()
    for s in (1, 2, 3):
        sum_in.pass_across(s)
    sum_in.finish()
    for copy in sum_out.twin + sum_gate.twin + sum_in.twin:
        copy.wait_recv()
    for copy in pending:
        copy.wait_send()


def wide_kernel(packed, output, grad_tokens, gout, ggate, gmix, *refs):
    out_o, out_t, gin_f, gout_f, *rows, wide_in, wide_out, value, sems = refs
    steps = wide_in.shape[0]
    cols, lines = wide_in.shape[2], wide_out.shape[1]
    copies = [
        pltpu.make_async_copy(output, out_o, sems.at[2, 0]),
        pltpu.make_async_copy(grad_tokens, out_t, sems.at[2, 1]),
    ]
    for copy in copies:
        copy.start()
    e, d = ggate.shape
    blocks = e // cols
    shards = 2 * TEAM
    zrows, stride = e // shards, gmix.shape[0] // shards
    per = shards // blocks

    def piece(n, first, last):
        return gmix[n * stride + first : n * stride + last, :]

    for i in range(steps):
        if i < blocks:
            turned = jnp.concatenate([piece(i * per + n, 0, zrows) for n in range(per)], axis=0).T
        else:
            turned = ggate[(i - blocks) * cols : (i - blocks + 1) * cols, :].T
        wide_in[i] = turned.astype(f32)
        at = slice(i * cols, (i + 1) * cols)
        copies.append(pltpu.make_async_copy(wide_in.at[i], gin_f.at[:, at], sems.at[0, i]))
        copies[-1].start()
        at = slice(i * lines, (i + 1) * lines)
        wide_out[i] = gout[at, :].astype(f32)
        copies.append(pltpu.make_async_copy(wide_out.at[i], gout_f.at[at, :], sems.at[1, i]))
        copies[-1].start()

    matrices = [ref for ref in rows if len(ref.shape) == 2]
    vectors = [ref for ref in rows if len(ref.shape) == 1]
    gain = 0.0
    tiles, across = d // LANES, packed // LANES
    for core in range(2):
        for n in range(value.shape[0] // 16 * tiles):
            first = (core * TEAM + n // across) * stride + zrows
            at_row, at_lane, lane = n // tiles * 16, n % tiles * LANES, n % across * LANES
            value[at_row : at_row + 16, at_lane : at_lane + LANES] = gmix[
                first : first + 16, lane : lane + LANES
            ].astype(f32)
        at_lanes = slice(core * d, (core + 1) * d)
        at = 0
        for ref in matrices:
            ref[:, at_lanes] = value[at : at + ref.shape[0], :]
            at += ref.shape[0]
        for ref in vectors[:-1]:
            ref[at_lanes] = value[at : at + 1, :].reshape(d)
            at += 1
        gain = gain + value[at : at + 1, :]
    vectors[-1][...] = gain.reshape(d)
    for copy in copies:
        copy.wait()


def local(
    tokens, marks, norm_gain, in_weight, conv_weight, conv_bias, x_weight, dt_weight,
    dt_bias, a_log, skip, out_weight, cotangent,
):
    tl, d = tokens.shape[1:]
    e = out_weight.shape[0]
    w = e // lax.axis_size("seq")
    t = tl * lax.axis_size("seq")
    states, rank, nproj, taps = a_log.shape[0], dt_weight.shape[0], x_weight.shape[0], conv_weight.shape[0]
    chunks, span = t // STEP, STEP * states
    quarter = w // PLANE
    zrows = quarter // DEPTH
    lines = -(-(nproj + rank + states + taps + 4) // 16) * 16
    packed = -(-(lines // 16) * (w // LANES) // TEAM) * LANES
    small = 16 * TEAM
    srows = zrows + 16
    vmem = pl.BlockSpec(memory_space=pltpu.VMEM)
    anywhere = pl.BlockSpec(memory_space=pl.ANY)
    wide = pltpu.VMEM((t, w), f32)
    low = pltpu.VMEM((t, w), bf16)
    one = pltpu.VMEM((t, LANES), f32)
    scratch = [
        pltpu.VMEM((d, w), bf16), pltpu.VMEM((d, w), bf16), pltpu.VMEM((w, d), bf16),
        pltpu.VMEM((d,), f32), pltpu.VMEM((taps, w), f32), pltpu.VMEM((e,), f32),
        pltpu.VMEM((nproj, w), bf16), pltpu.VMEM((rank, w), bf16), pltpu.VMEM((e,), f32),
        pltpu.VMEM((states, w), f32), pltpu.VMEM((e,), f32), pltpu.VMEM((8, tl), jnp.int32),
        pltpu.VMEM((3, t, d), bf16), pltpu.VMEM((PLANE - 1, 2, t, d), bf16),
        pltpu.VMEM((8, t), f32), pltpu.VMEM((t + 8, LANES), f32), pltpu.VMEM((8, e), f32),
        pltpu.VMEM((t + 8, w), f32), wide, wide, wide, wide, low, wide, wide, wide, wide, wide, wide, wide,
        one, one, one, one, pltpu.VMEM((LANES, t), f32),
        pltpu.VMEM((t * states // 2, w), bf16), pltpu.VMEM((t * states // 2 + states, w), bf16),
        pltpu.VMEM((chunks, states, LANES), f32), pltpu.VMEM((chunks, states, LANES), f32),
        pltpu.VMEM((t, span), bf16), pltpu.VMEM((t, span), bf16),
        *[pltpu.VMEM((span, w), bf16)] * 4, *[pltpu.VMEM((span, LANES), bf16)] * 4,
        *[pltpu.VMEM((chunks, states, LANES), f32)] * 2,
        pltpu.VMEM((states, LANES), f32), pltpu.VMEM((taps + 3, 8, w), f32),
        low, low, low, low, pltpu.VMEM((3, w, t), bf16), pltpu.VMEM((t + 8, w), f32),
        pltpu.VMEM((t, d), f32), pltpu.VMEM((tl, d), f32),
        pltpu.VMEM((t, d), f32), pltpu.VMEM((tl, d), f32),
        pltpu.VMEM((3, PLANE - 1, quarter, t), bf16), pltpu.VMEM((quarter, d), f32),
        pltpu.VMEM((3, zrows, d), f32), pltpu.VMEM((3, quarter, d), bf16),
        pltpu.VMEM((3, DEPTH - 1, zrows, d), bf16),
        pltpu.VMEM((lines, w), f32), pltpu.VMEM((small, packed), bf16), pltpu.VMEM((small, packed), f32),
        pltpu.VMEM((PLANE - 1, small // PLANE, packed), bf16), pltpu.VMEM((small // PLANE, packed), bf16),
        pltpu.VMEM((DEPTH - 1, 16, packed), bf16),
        pltpu.SemaphoreType.DMA((16,)),
        pltpu.SemaphoreType.DMA((128,)), pltpu.SemaphoreType.DMA((128,)),
    ]
    output, grad_tokens, gout, ggate, gmix = pl.pallas_call(
        body_kernel,
        out_shape=[
            pltpu.VMEM((tl, d), bf16),
            pltpu.VMEM((tl, d), bf16),
            pltpu.VMEM((e, d), bf16),
            pltpu.VMEM((e, d), bf16),
            pltpu.VMEM((2 * TEAM * srows, d), bf16),
        ],
        in_specs=[anywhere] * 13,
        out_specs=[vmem] * 5,
        scratch_shapes=scratch,
        compiler_params=pltpu.CompilerParams(
            collective_id=0, has_side_effects=True, vmem_limit_bytes=56 * 2**20
        ),
        name="block",
    )(
        tokens.reshape(tl, d), marks.reshape(1, tl), norm_gain, in_weight, conv_weight,
        conv_bias, x_weight, dt_weight, dt_bias, a_log, skip, out_weight, cotangent.reshape(tl, d),
    )

    steps = 8
    shapes = [(nproj, e), (rank, e), (states, e), (taps, e), (e,), (e,), (e,), (d,)]
    wide_shapes = [jax.ShapeDtypeStruct(s, f32) for s in [(d, 2 * e), (e, d)] + shapes]
    output, grad_tokens, *grads = pl.pallas_call(
        functools.partial(wide_kernel, packed),
        out_shape=[jax.ShapeDtypeStruct((tl, d), bf16)] * 2 + wide_shapes,
        in_specs=[vmem] * 5,
        out_specs=[anywhere] * 4 + [vmem] * len(shapes),
        scratch_shapes=[
            pltpu.VMEM((steps, d, 2 * e // steps), f32),
            pltpu.VMEM((steps, e // steps, d), f32),
            pltpu.VMEM((lines, w), f32),
            pltpu.SemaphoreType.DMA((3, steps)),
        ],
        compiler_params=pltpu.CompilerParams(vmem_limit_bytes=40 * 2**20),
        name="widen",
    )(output, grad_tokens, gout, ggate, gmix)
    rows = lax.axis_size("rows")
    if rows > TEAM:
        grads = [v * (1.0 / TEAM) for v in lax.psum(grads, "rows")]
    grad_in, grad_out, grad_x, grad_dt, grad_log, grad_conv, g_cb, g_dtb, g_skip, g_gain = grads
    return (
        output[None], grad_tokens[None], g_gain, grad_in, grad_conv, g_cb, grad_x, grad_dt, g_dtb, grad_log,
        g_skip, grad_out,
    )


def solution(mesh):
    split = P("rows", "seq", None)
    whole = P()
    in_specs = (split, P("rows", "seq")) + (whole,) * 10 + (split,)
    out_specs = (split, split) + (whole,) * 10
    return jax.shard_map(local, mesh=mesh, in_specs=in_specs, out_specs=out_specs, check_vma=False)
```

time: 106 us -> 88.2 us (0.83)
  Pallas kernels: 104 us -> 87.4 us
  local copies, waits for them, and re-layouts: 1.36 us -> 0 us
    pallas_call x2, Pallas kernels: 104 us -> 87.4 us  [the longest x1 81 us: local(): pl.pallas_call(body_kernel, out_shape=[pltpu.VMEM((tl, d), bf16), pltpu.V...]
    unnamed x6 -> x0, local copies, waits for them, and re-layouts: 1.36 us -> none
where the time goes in v2:
time: 88.2 us; the launch traced here: 88 us
  Pallas kernels  87.4 us (99%)
    pallas_call x1, Pallas kernels, local(): pl.pallas_call(body_kernel, out_shape=[pltpu.VMEM((tl, d), bf16), pltpu.V...  81 us
    pallas_call x1, Pallas kernels, local(): pl.pallas_call(functools.partial(wide_kernel, packed), out_shape=[jax.Sha...  6.37 us

profile of v2, /device:TPU:1, one launch (start us, length us, event | category | flops | bytes accessed | tf_op | source)
XLA Modules:
  0.0 88.0 jit_solution(18037506500687924638)
XLA Ops:
  0.6 81.0 %block.1 = (bf16[128,768]{1,0:T(8,128)(2,1)S(1)}, bf16[128,768]{1,0:T(8,128)(2,1)S(1)}, bf16[1536,768]{1,0:T(8,128)(2,1)S(1)}, bf16[1536,768]{1,0:T(8,128)(2,1)S(1)}, bf16[2048,768]{1,0:T(8,128)(2,1)S(1)}) custom-call(bf16[128,768]{1,0:T(8,128)(2,1)} %bitcast.4, s32[1,128]{1,0:T(1,128)} %marks.1, f32[768]{0:T(1024)} %gain_in.1, bf16[768,3072]{1,0:T(8,128)(2,1)} %win.1, ...), custom_call_target="tpu_custom_call" | custom-call | tf_op jit(solution)/shard_map/block/pallas_call | solution.py:900
  81.7 6.4 %widen.1 = (bf16[128,768]{1,0:T(8,128)(2,1)}, bf16[128,768]{1,0:T(8,128)(2,1)}, f32[768,3072]{1,0:T(8,128)}, f32[1536,768]{1,0:T(8,128)}, f32[80,1536]{1,0:T(8,1...) custom-call(bf16[128,768]{1,0:T(8,128)(2,1)S(1)} %get-tuple-element., ...), custom_call_target="tpu_custom_call" | custom-call | tf_op jit(solution)/shard_map/widen/pallas_call | solution.py:924

commit v3 on v2

--- a/solution.py
+++ b/solution.py
@@ -182,7 +182,7 @@
             ng[0, at, :] = (rows * scale * gain_row).astype(bf16)
             return carry
 
-        lax.fori_loop(0, tl // unit, norm_block, 0)
+        lax.fori_loop(0, tl // unit, norm_block, 0, unroll=4)
 
     norm_rows(mine)
     share(0)
@@ -252,7 +252,7 @@
             dsilu[pl.ds(at, STEP), sl] = sg * (1.0 + total * (1.0 - sg))
         return carry
 
-    lax.fori_loop(0, chunks, conv_block, 0)
+    lax.fori_loop(0, chunks, conv_block, 0, unroll=4)
     xw_own = xw[...]
     pp[:, 0:nproj] = mm(actl[...], xw_own, NT)
     proj_copy = Send(lambda: (pp, pq), row, other)
@@ -269,7 +269,7 @@
             dyf[at, sl] = low.astype(f32)
         return carry
 
-    lax.fori_loop(0, chunks, dy_block, 0)
+    lax.fori_loop(0, chunks, dy_block, 0, unroll=4)
 
     share_on(1)
 
@@ -303,7 +303,7 @@
             ddec[at, sl] = jnp.where(marked, 1e30, delta)
         return carry
 
-    lax.fori_loop(0, chunks, delta_block, 0)
+    lax.fori_loop(0, chunks, delta_block, 0, unroll=4)
 
     span = STEP * states
     pick = (
@@ -467,7 +467,7 @@
     sum_out, sum_gate, sum_in = Sum(0, gt), Sum(1, dgl), Sum(2, dil)
 
     def gated_half(part):
-        lax.fori_loop(part * chunks // 2, (part + 1) * chunks // 2, gated_block, 0)
+        lax.fori_loop(part * chunks // 2, (part + 1) * chunks // 2, gated_block, 0, unroll=4)
         sum_out.send_factors(part)
 
     pairs = chunks // 2
@@ -491,8 +491,6 @@
     read_chunk(chunks - 1, odd, odd_at(pairs - 1))
     gated_half(1)
     share_end(1)
-    sum_gate.send_factors(0)
-    sum_gate.send_factors(1)
 
     late = sum(dyf[t - 1 : t, sl] * final[j] for j, sl in enumerate(tile))
     lastc[...] = jnp.broadcast_to(jnp.sum(late, axis=1, keepdims=True), (states, LANES))
@@ -583,7 +581,7 @@
     def projection_grads(part):
         at = slice(part * tl, (part + 1) * tl)
         span_of = (part * chunks // 2, (part + 1) * chunks // 2)
-        sums, gains = lax.fori_loop(*span_of, dpre_block, (read_tot(tot_dtb), read_tot(tot_skip)))
+        sums, gains = lax.fori_loop(*span_of, dpre_block, (read_tot(tot_dtb), read_tot(tot_skip)), unroll=4)
         write_tot(tot_dtb, sums)
         write_tot(tot_skip, gains)
         for k in range(*span_of):
@@ -637,10 +635,10 @@
         for sl in lane_tiles(w, 2 * LANES):
             sq[at, sl] = mm(dproj_low, xw[:, sl])
         names = range(tot_conv, tot_conv + taps + 1)
-        sums = lax.fori_loop(*span_of, dconv_block, tuple(read_tot(n) for n in names))
+        sums = lax.fori_loop(*span_of, dconv_block, tuple(read_tot(n) for n in names), unroll=4)
         for n, values in zip(names, sums):
             write_tot(n, values)
-        lax.fori_loop(*span_of, dinner_block, 0)
+        lax.fori_loop(*span_of, dinner_block, 0, unroll=4)
         sum_in.send_factors(part)
 
     def late_half():
@@ -652,18 +650,23 @@
             copy.wait_recv()
         sum_out.partial()
 
+    def gate_factors():
+        sum_gate.send_factors(0)
+        sum_gate.send_factors(1)
+
     def gate_sums():
         for copy in relays[0]:
             copy.wait_recv()
         sum_gate.partial()
 
+    def end_normed():
+        share_end(0)
+
+    def inner_late():
+        inner_grads(1)
+
     events = (
-        (1, lambda: share_end(0)),
-        (2, out_sums),
-        (3, late_half),
-        (5, gate_sums),
-        (6, lambda: inner_grads(1)),
-        (7, lambda: sum_out.total()),
+        (1, out_sums, gate_factors), (2, end_normed), (3, late_half), (5, gate_sums, sum_out.total), (6, inner_late),
     )
 
     def back_pair(step, carry):
@@ -672,8 +675,13 @@
         carry = back_chunk(2 * m + 1, carry, odd, odd_at(m), even, even_at(m) + span - states, *odd_bufs)
         back_sums(2 * m + 1, *odd_bufs)
         flow, acc = back_chunk(2 * m, carry, even, even_at(m), odd, even_at(m), *even_bufs)
-        for when, event in events:
-            pl.when(step == when * pairs // 8)(event)
+        for when, *steps in events:
+
+            @pl.when(step == when * pairs // 8)
+            def _():
+                for event in steps:
+                    event()
+
         return tuple(flow), tuple(acc)
 
     carry = lax.fori_loop(0, pairs, back_pair, (zeros, zeros))
@@ -711,7 +719,7 @@
         both = dn[rows, :] * (values * scale)
         return carry + both[0:8] + both[8:16]
 
-    total = lax.fori_loop(0, chunks, gain_block, jnp.zeros((8, d), f32))
+    total = lax.fori_loop(0, chunks, gain_block, jnp.zeros((8, d), f32), unroll=4)
     sm[line_gain : line_gain + 1, :] = jnp.sum(total, axis=0, keepdims=True)
     across_tiles = packed // LANES
     for n in range(sm.shape[0] // 16 * tiles):
@@ -750,6 +758,7 @@
     sum_out.pass_across(3)
     sum_gate.pass_on(3)
 
+    sum_in.total()
     for sl in lane_tiles(d, 2 * LANES):
         outp[:, sl] = mm(gt[...], wo[:, sl])
     out_copy = Send(lambda: (outp.at[pl.ds(theirs, tl), :], outr), row, other)
@@ -767,11 +776,10 @@
         return carry
 
     dn_copy.wait_recv()
-    lax.fori_loop(0, tl // STEP, norm_back, 0)
+    lax.fori_loop(0, tl // STEP, norm_back, 0, unroll=4)
     out_copy.wait_recv()
-    lax.fori_loop(0, tl // STEP, out_block, 0)
-
-    sum_in.total()
+    lax.fori_loop(0, tl // STEP, out_block, 0, unroll=4)
+
     sum_gate.pass_across(0)
     sum_gate.pass_across(1)
     sum_out.finish()
@@ -792,37 +800,37 @@
 
 
 def wide_kernel(packed, output, grad_tokens, gout, ggate, gmix, *refs):
-    out_o, out_t, gin_f, gout_f, *rows, wide_in, wide_out, value, sems = refs
+    out_o, out_t, gin_f, gout_f, *rest = refs
+    *rest, wide_in, wide_out, value, sems = rest
+    finals, rows = rest[: len(rest) // 2], rest[len(rest) // 2 :]
     steps = wide_in.shape[0]
     cols, lines = wide_in.shape[2], wide_out.shape[1]
-    copies = [
-        pltpu.make_async_copy(output, out_o, sems.at[2, 0]),
-        pltpu.make_async_copy(grad_tokens, out_t, sems.at[2, 1]),
-    ]
-    for copy in copies:
-        copy.start()
+    copies = []
+
+    def put(src, dst, *sem):
+        copies.append(pltpu.make_async_copy(src, dst, sems.at[sem]))
+        copies[-1].start()
+
+    put(output, out_o, 2, 0)
+    put(grad_tokens, out_t, 2, 1)
     e, d = ggate.shape
     blocks = e // cols
     shards = 2 * TEAM
     zrows, stride = e // shards, gmix.shape[0] // shards
     per = shards // blocks
 
-    def piece(n, first, last):
-        return gmix[n * stride + first : n * stride + last, :]
+    def inner_rows(i):
+        parts = [gmix[n * stride : n * stride + zrows, :] for n in range(i * per, (i + 1) * per)]
+        return jnp.concatenate(parts, axis=0)
 
     for i in range(steps):
-        if i < blocks:
-            turned = jnp.concatenate([piece(i * per + n, 0, zrows) for n in range(per)], axis=0).T
-        else:
-            turned = ggate[(i - blocks) * cols : (i - blocks + 1) * cols, :].T
-        wide_in[i] = turned.astype(f32)
-        at = slice(i * cols, (i + 1) * cols)
-        copies.append(pltpu.make_async_copy(wide_in.at[i], gin_f.at[:, at], sems.at[0, i]))
-        copies[-1].start()
         at = slice(i * lines, (i + 1) * lines)
         wide_out[i] = gout[at, :].astype(f32)
-        copies.append(pltpu.make_async_copy(wide_out.at[i], gout_f.at[at, :], sems.at[1, i]))
-        copies[-1].start()
+        put(wide_out.at[i], gout_f.at[at, :], 1, i)
+        gate_rows = slice((i - blocks) * cols, (i - blocks + 1) * cols)
+        turned = (inner_rows(i) if i < blocks else ggate[gate_rows, :]).T
+        wide_in[i] = turned.astype(f32)
+        put(wide_in.at[i], gin_f.at[:, i * cols : (i + 1) * cols], 0, i)
 
     matrices = [ref for ref in rows if len(ref.shape) == 2]
     vectors = [ref for ref in rows if len(ref.shape) == 1]
@@ -845,6 +853,8 @@
             at += 1
         gain = gain + value[at : at + 1, :]
     vectors[-1][...] = gain.reshape(d)
+    for n, (src, dst) in enumerate(zip(rows, finals)):
+        put(src, dst, 3, n)
     for copy in copies:
         copy.wait()
 
@@ -925,12 +935,13 @@
         functools.partial(wide_kernel, packed),
         out_shape=[jax.ShapeDtypeStruct((tl, d), bf16)] * 2 + wide_shapes,
         in_specs=[vmem] * 5,
-        out_specs=[anywhere] * 4 + [vmem] * len(shapes),
-        scratch_shapes=[
+        out_specs=[anywhere] * (4 + len(shapes)),
+        scratch_shapes=[pltpu.VMEM(s, f32) for s in shapes]
+        + [
             pltpu.VMEM((steps, d, 2 * e // steps), f32),
             pltpu.VMEM((steps, e // steps, d), f32),
             pltpu.VMEM((lines, w), f32),
-            pltpu.SemaphoreType.DMA((3, steps)),
+            pltpu.SemaphoreType.DMA((4, steps)),
         ],
         compiler_params=pltpu.CompilerParams(vmem_limit_bytes=40 * 2**20),
         name="widen",

time: 88.2 us -> 85.6 us (0.971)
  Pallas kernels: 87.4 us -> 84.8 us
    pallas_call x1, Pallas kernels: 81 us -> 79 us  [local(): pl.pallas_call(body_kernel, out_shape=[pltpu.VMEM((tl, d), bf16), pltpu.V...]
where the time goes in v3:
time: 85.6 us; the launch traced here: 85.4 us
  Pallas kernels  84.8 us (99%)
    pallas_call x1, Pallas kernels, local(): pl.pallas_call(body_kernel, out_shape=[pltpu.VMEM((tl, d), bf16), pltpu.V...  79 us
    pallas_call x1, Pallas kernels, local(): pl.pallas_call(functools.partial(wide_kernel, packed), out_shape=[jax.Sha...  5.73 us

profile of v3, /device:TPU:1, one launch (start us, length us, event | category | flops | bytes accessed | tf_op | source)
XLA Modules:
  0.0 85.4 jit_solution(5468766303982431063)
XLA Ops:
  0.6 79.0 %block.1 = (bf16[128,768]{1,0:T(8,128)(2,1)S(1)}, bf16[128,768]{1,0:T(8,128)(2,1)S(1)}, bf16[1536,768]{1,0:T(8,128)(2,1)S(1)}, bf16[1536,768]{1,0:T(8,128)(2,1)S(1)}, bf16[2048,768]{1,0:T(8,128)(2,1)S(1)}) custom-call(bf16[128,768]{1,0:T(8,128)(2,1)} %bitcast.4, s32[1,128]{1,0:T(1,128)} %marks.1, f32[768]{0:T(1024)} %gain_in.1, bf16[768,3072]{1,0:T(8,128)(2,1)} %win.1, ...), custom_call_target="tpu_custom_call" | custom-call | tf_op jit(solution)/shard_map/block/pallas_call | solution.py:910
  79.7 5.7 %widen.1 = (bf16[128,768]{1,0:T(8,128)(2,1)}, bf16[128,768]{1,0:T(8,128)(2,1)}, f32[768,3072]{1,0:T(8,128)}, f32[1536,768]{1,0:T(8,128)}, f32[80,1536]{1,0:T(8,1...) custom-call(bf16[128,768]{1,0:T(8,128)(2,1)S(1)} %get-tuple-element., ...), custom_call_target="tpu_custom_call" | custom-call | tf_op jit(solution)/shard_map/widen/pallas_call | solution.py:934

commit v4 on v3

--- a/solution.py
+++ b/solution.py
@@ -1,5 +1,3 @@
-import functools
-
 import jax
 import jax.numpy as jnp
 from jax import lax
@@ -30,7 +28,7 @@
 
 def body_kernel(
     tok, marks, gain_in, win, cw_in, cb_in, xw_in, dtw_in, dtb_in, alog_in, skip_in, wout, cot,
-    out, gtok, gout, ggate, gmix,
+    out, gtok, gout, ggate, ginner, small,
     win_i, win_g, wo, gain, cw, cb, xw, dtw, dtb, alog, skip, mkraw, ng, ngh, mk, mcol, lines,
     inner, gate, dgated, act, dsilu, actl, ddec, u, sig, dyf, du, s1, sq,
     pp, pq, pp2, pq2, tsc, even, odd, bt, ct, cbd, bbd, ga, gb, qa, qb, ba, bb, ca, cc, dbt, dct, lastc, tot,
@@ -365,7 +363,6 @@
     class Sum:
         def __init__(self, n, source):
             self.n, self.source, self.factors = n, source, []
-            self.lines = zrows + (extra if n == 2 else 0)
             self.near, self.far, self.twin = [], [], []
 
         def send_factors(self, part):
@@ -380,12 +377,12 @@
                 self.factors.append(Send(refs, plane_row[s], core))
 
         def rows(self, where, first, count):
-            ref = (gout, ggate, gmix)[self.n]
-            first = (core * PLANE + where) * DEPTH * self.lines + first
+            ref = (gout, ggate, ginner)[self.n]
+            first = chan + where * quarter + first
             return ref.at[pl.ds(pl.multiple_of(first, count), count), :]
 
         def shard(self, where, z):
-            return self.rows(where, z * self.lines, self.lines)
+            return self.rows(where, z * zrows, zrows)
 
         def partial(self):
             n = self.n
@@ -420,15 +417,7 @@
             for s in range(DEPTH - 1):
                 total = total + zr[self.n, s].astype(f32)
             part = self.shard(place, pz)
-            part[0:zrows, :] = total.astype(bf16)
-            if self.n == 2:
-                for copy in small_depth:
-                    copy.wait_recv()
-                total = sms[block(place * DEPTH + pz, extra), :]
-                for s in range(DEPTH - 1):
-                    total = total + szr[s].astype(f32)
-                part[zrows:, 0:packed] = total.astype(bf16)
-                part[zrows:, packed:] = jnp.zeros((extra, d - packed), bf16)
+            part[...] = total.astype(bf16)
             own = pair_to(lambda: self.shard(place, pz))
             self.along = [Send(own, z_row[s], core) for s in (1, 2)]
             self.beyond = []
@@ -449,20 +438,24 @@
         def pass_across(self, s):
             for copy in self.near[s]:
                 copy.wait_recv()
-            q = 1 + s % 2
-            part = pair_to(lambda: self.shard(plane_place[q], z_place[s]))
-            self.far.append(Send(part, plane_row[3 - q], core))
+            far = []
+            for q in (1, 2):
+                part = pair_to(lambda q=q: self.shard(plane_place[q], z_place[s]).at[:, halves[q - 1]])
+                far.append(Send(part, plane_row[3 - q], core))
+            self.far.append(far)
             if s == DEPTH - 1:
                 for q in (1, 2):
                     self.to_twin(plane_place[q])
 
         def to_twin(self, where):
-            self.twin.append(Send(pair_to(lambda: self.rows(where, 0, DEPTH * self.lines)), row, other))
+            self.twin.append(Send(pair_to(lambda: self.rows(where, 0, quarter)), row, other))
 
         def finish(self):
-            for copy in self.far:
-                copy.wait_recv()
-            self.to_twin(plane_place[3])
+            for s, far in enumerate(self.far):
+                for copy in far:
+                    copy.wait_recv()
+                part = pair_to(lambda s=s: self.shard(plane_place[3], z_place[s]))
+                self.twin.append(Send(part, row, other))
 
     sum_out, sum_gate, sum_in = Sum(0, gt), Sum(1, dgl), Sum(2, dil)
 
@@ -756,9 +749,23 @@
     sum_out.pass_across(1)
     sum_out.pass_across(2)
     sum_out.pass_across(3)
+    for copy in small_depth:
+        copy.wait_recv()
+
+    def small_rows(first, count):
+        first = (core * TEAM + first) * extra
+        return small.at[pl.ds(pl.multiple_of(first, count * extra), count * extra), :]
+
+    own_small = place * DEPTH + pz
+    total = sms[block(own_small, extra), :]
+    for s in range(DEPTH - 1):
+        total = total + szr[s].astype(f32)
+    small_rows(own_small, 1)[...] = total.astype(bf16)
+    refs = pair_to(lambda: small_rows(own_small, 1))
+    small_along = [Send(refs, z_row[s], core) for s in range(1, DEPTH)]
     sum_gate.pass_on(3)
-
     sum_in.total()
+
     for sl in lane_tiles(d, 2 * LANES):
         outp[:, sl] = mm(gt[...], wo[:, sl])
     out_copy = Send(lambda: (outp.at[pl.ds(theirs, tl), :], outr), row, other)
@@ -782,6 +789,10 @@
 
     sum_gate.pass_across(0)
     sum_gate.pass_across(1)
+    for copy in small_along:
+        copy.wait_recv()
+    refs = pair_to(lambda: small_rows(place * DEPTH, DEPTH))
+    small_near = [Send(refs, plane_row[s], core) for s in range(1, PLANE)]
     sum_out.finish()
     sum_in.pass_on(1)
     sum_in.pass_on(2)
@@ -789,17 +800,20 @@
     sum_gate.pass_across(3)
     sum_in.pass_on(3)
     sum_in.pass_across(0)
+    for copy in small_near:
+        copy.wait_recv()
+    twin_small = Send(pair_to(lambda: small_rows(0, TEAM)), row, other)
     sum_gate.finish()
     for s in (1, 2, 3):
         sum_in.pass_across(s)
     sum_in.finish()
-    for copy in sum_out.twin + sum_gate.twin + sum_in.twin:
+    for copy in sum_out.twin + sum_gate.twin + [twin_small] + sum_in.twin:
         copy.wait_recv()
     for copy in pending:
         copy.wait_send()
 
 
-def wide_kernel(packed, output, grad_tokens, gout, ggate, gmix, *refs):
+def wide_kernel(output, grad_tokens, gout, ggate, ginner, small, *refs):
     out_o, out_t, gin_f, gout_f, *rest = refs
     *rest, wide_in, wide_out, value, sems = rest
     finals, rows = rest[: len(rest) // 2], rest[len(rest) // 2 :]
@@ -815,32 +829,24 @@
     put(grad_tokens, out_t, 2, 1)
     e, d = ggate.shape
     blocks = e // cols
-    shards = 2 * TEAM
-    zrows, stride = e // shards, gmix.shape[0] // shards
-    per = shards // blocks
-
-    def inner_rows(i):
-        parts = [gmix[n * stride : n * stride + zrows, :] for n in range(i * per, (i + 1) * per)]
-        return jnp.concatenate(parts, axis=0)
-
     for i in range(steps):
         at = slice(i * lines, (i + 1) * lines)
         wide_out[i] = gout[at, :].astype(f32)
         put(wide_out.at[i], gout_f.at[at, :], 1, i)
-        gate_rows = slice((i - blocks) * cols, (i - blocks + 1) * cols)
-        turned = (inner_rows(i) if i < blocks else ggate[gate_rows, :]).T
-        wide_in[i] = turned.astype(f32)
+        source = ginner if i < blocks else ggate
+        first = i % blocks * cols
+        wide_in[i] = source[first : first + cols, :].T.astype(f32)
         put(wide_in.at[i], gin_f.at[:, i * cols : (i + 1) * cols], 0, i)
 
     matrices = [ref for ref in rows if len(ref.shape) == 2]
     vectors = [ref for ref in rows if len(ref.shape) == 1]
     gain = 0.0
-    tiles, across = d // LANES, packed // LANES
+    tiles, across = d // LANES, small.shape[1] // LANES
     for core in range(2):
         for n in range(value.shape[0] // 16 * tiles):
-            first = (core * TEAM + n // across) * stride + zrows
+            first = (core * TEAM + n // across) * 16
             at_row, at_lane, lane = n // tiles * 16, n % tiles * LANES, n % across * LANES
-            value[at_row : at_row + 16, at_lane : at_lane + LANES] = gmix[
+            value[at_row : at_row + 16, at_lane : at_lane + LANES] = small[
                 first : first + 16, lane : lane + LANES
             ].astype(f32)
         at_lanes = slice(core * d, (core + 1) * d)
@@ -873,8 +879,7 @@
     zrows = quarter // DEPTH
     lines = -(-(nproj + rank + states + taps + 4) // 16) * 16
     packed = -(-(lines // 16) * (w // LANES) // TEAM) * LANES
-    small = 16 * TEAM
-    srows = zrows + 16
+    pieces = 16 * TEAM
     vmem = pl.BlockSpec(memory_space=pltpu.VMEM)
     anywhere = pl.BlockSpec(memory_space=pl.ANY)
     wide = pltpu.VMEM((t, w), f32)
@@ -901,23 +906,24 @@
         pltpu.VMEM((3, PLANE - 1, quarter, t), bf16), pltpu.VMEM((quarter, d), f32),
         pltpu.VMEM((3, zrows, d), f32), pltpu.VMEM((3, quarter, d), bf16),
         pltpu.VMEM((3, DEPTH - 1, zrows, d), bf16),
-        pltpu.VMEM((lines, w), f32), pltpu.VMEM((small, packed), bf16), pltpu.VMEM((small, packed), f32),
-        pltpu.VMEM((PLANE - 1, small // PLANE, packed), bf16), pltpu.VMEM((small // PLANE, packed), bf16),
+        pltpu.VMEM((lines, w), f32), pltpu.VMEM((pieces, packed), bf16), pltpu.VMEM((pieces, packed), f32),
+        pltpu.VMEM((PLANE - 1, pieces // PLANE, packed), bf16), pltpu.VMEM((pieces // PLANE, packed), bf16),
         pltpu.VMEM((DEPTH - 1, 16, packed), bf16),
         pltpu.SemaphoreType.DMA((16,)),
-        pltpu.SemaphoreType.DMA((128,)), pltpu.SemaphoreType.DMA((128,)),
+        pltpu.SemaphoreType.DMA((160,)), pltpu.SemaphoreType.DMA((160,)),
     ]
-    output, grad_tokens, gout, ggate, gmix = pl.pallas_call(
+    output, grad_tokens, gout, ggate, ginner, small = pl.pallas_call(
         body_kernel,
         out_shape=[
             pltpu.VMEM((tl, d), bf16),
             pltpu.VMEM((tl, d), bf16),
             pltpu.VMEM((e, d), bf16),
             pltpu.VMEM((e, d), bf16),
-            pltpu.VMEM((2 * TEAM * srows, d), bf16),
+            pltpu.VMEM((e, d), bf16),
+            pltpu.VMEM((2 * TEAM * 16, packed), bf16),
         ],
         in_specs=[anywhere] * 13,
-        out_specs=[vmem] * 5,
+        out_specs=[vmem] * 6,
         scratch_shapes=scratch,
         compiler_params=pltpu.CompilerParams(
             collective_id=0, has_side_effects=True, vmem_limit_bytes=56 * 2**20
@@ -932,9 +938,9 @@
     shapes = [(nproj, e), (rank, e), (states, e), (taps, e), (e,), (e,), (e,), (d,)]
     wide_shapes = [jax.ShapeDtypeStruct(s, f32) for s in [(d, 2 * e), (e, d)] + shapes]
     output, grad_tokens, *grads = pl.pallas_call(
-        functools.partial(wide_kernel, packed),
+        wide_kernel,
         out_shape=[jax.ShapeDtypeStruct((tl, d), bf16)] * 2 + wide_shapes,
-        in_specs=[vmem] * 5,
+        in_specs=[vmem] * 6,
         out_specs=[anywhere] * (4 + len(shapes)),
         scratch_shapes=[pltpu.VMEM(s, f32) for s in shapes]
         + [
@@ -945,7 +951,7 @@
         ],
         compiler_params=pltpu.CompilerParams(vmem_limit_bytes=40 * 2**20),
         name="widen",
-    )(output, grad_tokens, gout, ggate, gmix)
+    )(output, grad_tokens, gout, ggate, ginner, small)
     rows = lax.axis_size("rows")
     if rows > TEAM:
         grads = [v * (1.0 / TEAM) for v in lax.psum(grads, "rows")]

time: 85.6 us -> 85.4 us (level)
  no operation moved by 1% of the time
where the time goes in v4:
time: 85.4 us; the launch traced here: 85.2 us
  Pallas kernels  84.6 us (99%)
    pallas_call x1, Pallas kernels, local(): pl.pallas_call(body_kernel, out_shape=[pltpu.VMEM((tl, d), bf16), pltpu.V...  78.9 us
    pallas_call x1, Pallas kernels, local(): pl.pallas_call(wide_kernel, out_shape=[jax.ShapeDtypeStruct((tl, d), bf16...  5.73 us

profile of v4, /device:TPU:1, one launch (start us, length us, event | category | flops | bytes accessed | tf_op | source)
XLA Modules:
  0.0 85.2 jit_solution(12117602821469368383)
XLA Ops:
  0.6 78.9 %block.1 = (bf16[128,768]{1,0:T(8,128)(2,1)S(1)}, bf16[128,768]{1,0:T(8,128)(2,1)S(1)}, bf16[1536,768]{1,0:T(8,128)(2,1)S(1)}, bf16[1536,768]{1,0:T(8,128)(2,1)S...) custom-call(bf16[128,768]{1,0:T(8,128)(2,1)} %bitcast.4, s32[1,128]{1,0:T(1,128)} %marks.1, ...), custom_call_target="tpu_custom_call" | custom-call | tf_op jit(solution)/shard_map/block/pallas_call | solution.py:915
  79.5 5.7 %widen.1 = (bf16[128,768]{1,0:T(8,128)(2,1)}, bf16[128,768]{1,0:T(8,128)(2,1)}, f32[768,3072]{1,0:T(8,128)}, f32[1536,768]{1,0:T(8,128)}, f32[80,1536]{1,0:T(8,1...) custom-call(bf16[128,768]{1,0:T(8,128)(2,1)S(1)} %get-tuple-element., ...), custom_call_target="tpu_custom_call" | custom-call | tf_op jit(solution)/shard_map/widen/pallas_call | solution.py:940

commit v5 on v4

--- a/solution.py
+++ b/solution.py
@@ -833,6 +833,7 @@
         at = slice(i * lines, (i + 1) * lines)
         wide_out[i] = gout[at, :].astype(f32)
         put(wide_out.at[i], gout_f.at[at, :], 1, i)
+    for i in range(steps):
         source = ginner if i < blocks else ggate
         first = i % blocks * cols
         wide_in[i] = source[first : first + cols, :].T.astype(f32)

time: 85.4 us -> 85.4 us (level)
  no operation moved by 1% of the time
where the time goes in v5:
time: 85.4 us; the launch traced here: 85.2 us
  Pallas kernels  84.6 us (99%)
    pallas_call x1, Pallas kernels, local(): pl.pallas_call(body_kernel, out_shape=[pltpu.VMEM((tl, d), bf16), pltpu.V...  78.9 us
    pallas_call x1, Pallas kernels, local(): pl.pallas_call(wide_kernel, out_shape=[jax.ShapeDtypeStruct((tl, d), bf16...  5.72 us

profile of v5, /device:TPU:1, one launch (start us, length us, event | category | flops | bytes accessed | tf_op | source)
XLA Modules:
  0.0 85.2 jit_solution(1631438553963945314)
XLA Ops:
  0.6 78.9 %block.1 = (bf16[128,768]{1,0:T(8,128)(2,1)S(1)}, bf16[128,768]{1,0:T(8,128)(2,1)S(1)}, bf16[1536,768]{1,0:T(8,128)(2,1)S(1)}, bf16[1536,768]{1,0:T(8,128)(2,1)S...) custom-call(bf16[128,768]{1,0:T(8,128)(2,1)} %bitcast.4, s32[1,128]{1,0:T(1,128)} %marks.1, ...), custom_call_target="tpu_custom_call" | custom-call | tf_op jit(solution)/shard_map/block/pallas_call | solution.py:916
  79.5 5.7 %widen.1 = (bf16[128,768]{1,0:T(8,128)(2,1)}, bf16[128,768]{1,0:T(8,128)(2,1)}, f32[768,3072]{1,0:T(8,128)}, f32[1536,768]{1,0:T(8,128)}, f32[80,1536]{1,0:T(8,1...) custom-call(bf16[128,768]{1,0:T(8,128)(2,1)S(1)} %get-tuple-element., ...), custom_call_target="tpu_custom_call" | custom-call | tf_op jit(solution)/shard_map/widen/pallas_call | solution.py:941
